TPU v7x, 32 devices: a whole 2x2x4 slice. The times are simulated.
32 devices in a mesh: fsdp: 2 (over x), tok: 16 (over z, y, core).
Axes of the slice: x: 2, y: 2, z: 4, core: 2. Of those that a mesh axis runs over, the one named last changes fastest.
Arguments:
- queries: bfloat16 [2, 2048, 3072], P('fsdp', 'tok'), may hold values from -6 to 6
- keys: bfloat16 [2, 2048, 3072], P('fsdp', 'tok'), may hold values from -6 to 6
- values: bfloat16 [2, 2048, 3072], P('fsdp', 'tok'), may hold values from -6 to 6
- readout: bfloat16 [3072, 1000], P('fsdp'), may hold values from -12 to 12
- global_block: int32 [2], P('fsdp'), may hold values from 0 to 15
- q_gain: float32 [3072], replicated, may hold values from 0.5 to 5
- k_gain: float32 [3072], replicated, may hold values from 0.5 to 5
Outputs:
- entropy: float32 [], replicated
- q_grad: float32 [3072], replicated
- k_grad: float32 [3072], replicated
All inputs are finite; a program needn't handle non-finite values.
Results may differ from a plain program's by a relative error of at most 0.02.
The roundings to bfloat16 on the way count: a program that leaves them out, or rounds other values in their place, can miss the bound.
Values may be sent and summed in bfloat16 or wider, within the bound.
No kernel may reach another device: no remote copies, remote signals or barrier semaphores. Data moves between devices by JAX's collectives and lax.ppermute only.
A program may use at most 64 MiB of HBM per device.

v0:
```python
import jax
import jax.numpy as jnp
from jax import lax
from jax.sharding import PartitionSpec as P

HEAD = 128
ROW = 64
GBLK = 128


score_entries = 1 << 20


def with_halo(x, sides, width):
    for axis, dim in sides:
        peers, length = (lax.axis_size(axis), x.shape[dim])
        up = [(i, (i + 1) % peers) for i in range(peers - 1)]
        down = [(j, i) for i, j in up]
        last = lax.slice_in_dim(x, length - width, length, axis=dim)
        first = lax.slice_in_dim(x, 0, width, axis=dim)
        before = lax.ppermute(last, axis, up)
        after = lax.ppermute(first, axis, down)
        x = jnp.concatenate([before, x, after], axis=dim)
    return x


def broadcast(block, axis, holder):
    block = jnp.where(lax.axis_index(axis) == holder, block, jnp.zeros_like(block))
    return lax.psum(block, axis)


def normalize(entries, gain):
    entries = entries.astype(jnp.float32)
    average = jnp.mean(entries, -1, keepdims=True)
    centred = entries - average
    variance = jnp.mean(centred * centred, -1, keepdims=True)
    return (centred * lax.rsqrt(variance + 1e-06) * gain).astype(jnp.bfloat16)


def group_total(query_part, key_part, value_part, usable, gain_query, gain_key):
    query_norm = normalize(query_part, gain_query)
    key_norm = normalize(key_part, gain_key)
    scores = jnp.einsum(
        "qhd,khd->hqk", query_norm, key_norm, preferred_element_type=jnp.float32
    ) * HEAD ** (-0.5)
    scores = jnp.where(usable[None, None, :], scores, -1e30)
    row_max = jnp.max(scores, -1, keepdims=True)
    exponent = jnp.exp(scores - row_max)
    row_total = jnp.sum(exponent, -1, keepdims=True)
    attention = (exponent / row_total).astype(jnp.bfloat16)
    return jnp.einsum("hqk,khd->hd", attention, value_part, preferred_element_type=jnp.float32)


def pick_group(head_count, row_count, key_count):
    chosen_size = 1
    for candidate in range(1, head_count + 1):
        if head_count % candidate == 0 and candidate * row_count * key_count <= score_entries:
            chosen_size = candidate
    return chosen_size


def attend_sum(query_rows, context, usable, gain_query, gain_key, group_size):
    head_count = gain_query.shape[0] // HEAD
    query_heads = query_rows.reshape(query_rows.shape[0], head_count, HEAD)
    key_heads = context[0].reshape(context.shape[1], head_count, HEAD)
    value_heads = context[1].reshape(context.shape[1], head_count, HEAD)
    query_gains = gain_query.reshape(head_count, HEAD)
    key_gains = gain_key.reshape(head_count, HEAD)
    checked = jax.checkpoint(group_total)

    def per_group(group_index):
        first_head = group_index * group_size
        return checked(
            lax.dynamic_slice_in_dim(query_heads, first_head, group_size, 1),
            lax.dynamic_slice_in_dim(key_heads, first_head, group_size, 1),
            lax.dynamic_slice_in_dim(value_heads, first_head, group_size, 1),
            usable,
            lax.dynamic_slice_in_dim(query_gains, first_head, group_size, 0),
            lax.dynamic_slice_in_dim(key_gains, first_head, group_size, 0),
        )

    return lax.map(per_group, jnp.arange(head_count // group_size, dtype=jnp.int32)).reshape(-1)


def body(queries, keys, values, readout, global_block, q_gain, k_gain):
    tok_count = lax.axis_size("tok")
    view_count = lax.axis_size("fsdp")
    position = lax.axis_index("tok")
    query_rows = queries[0]
    tok_dev = query_rows.shape[0]
    view_tokens = tok_dev * tok_count
    key_value = jnp.stack([keys[0], values[0]])
    padded = with_halo(key_value, (("tok", 1),), ROW)
    lower_rows = padded[:, :ROW]
    upper_rows = padded[:, ROW + tok_dev :]
    global_id = global_block[0]
    per_device = tok_dev // GBLK
    owner_index = global_id // per_device
    shared = broadcast(key_value, "tok", owner_index)
    context = jnp.concatenate([key_value, lower_rows, upper_rows, shared], axis=1)
    usable = jnp.concatenate(
        [
            jnp.ones((tok_dev,), bool),
            jnp.full((ROW,), position > 0),
            jnp.full((ROW,), position < tok_count - 1),
            jnp.ones((GBLK,), bool),
        ]
    )
    group_size = pick_group(q_gain.shape[0] // HEAD, tok_dev, context.shape[1])

    def local_total(gain_query, gain_key):
        return attend_sum(query_rows, context, usable, gain_query, gain_key, group_size)

    band_total, pullback = jax.vjp(local_total, q_gain, k_gain)
    pooled = lax.psum(band_total, "tok") / view_tokens
    weight = lax.all_gather(readout, "fsdp", axis=0, tiled=True).astype(jnp.float32)
    logits = jnp.dot(pooled, weight, precision=lax.Precision.HIGHEST)
    view_probs = jax.nn.softmax(logits, -1)
    mean_probs = lax.psum(view_probs, "fsdp") / view_count
    entropy = -jnp.sum(mean_probs * jnp.log(mean_probs))
    upstream = -(jnp.log(mean_probs) + 1.0) / view_count
    dlogits = view_probs * (upstream - jnp.sum(view_probs * upstream))
    dpooled = jnp.dot(weight, dlogits, precision=lax.Precision.HIGHEST)
    query_grad, key_grad = pullback(dpooled / view_tokens)
    query_grad, key_grad = lax.psum((query_grad, key_grad), ("fsdp", "tok"))
    return (entropy, query_grad, key_grad)


def solution(mesh):
    in_specs = (
        P("fsdp", "tok", None),
        P("fsdp", "tok", None),
        P("fsdp", "tok", None),
        P("fsdp", None),
        P("fsdp"),
        P(),
        P(),
    )
    out_specs = (P(), P(), P())
    return jax.shard_map(body, mesh=mesh, in_specs=in_specs, out_specs=out_specs, check_vma=False)
```

profile of v0, /device:TPU:0, one launch (start us, length us, event | category | flops | bytes accessed | tf_op | source)
XLA Modules:
  0.0 325.8 jit_solution(7031780769092431224)
XLA Ops:
  14.8 2.4 copy.24
  17.2 3.3 %collective-permute-start = (bf16[2,64,3072]{2,1,0:T(8,128)(2,1)}, bf16[2,64,3072]{2,1,0:T(8,128)(2,1)}, u32[]{:S(2)}, u32[]{:S(2)}) collective-permute-start(bf16[2,64,3072]{2,1,0:T(8,128)(2,1)} %copy.24), channel_id=1, source_target_pairs={{0,1},{1,2},{2,3},{3,4},{4,5},{5,6},{6,7},{7,8},{8,9},{9,10},{10,1... | collective-permute-start | bytes 2359304 | tf_op jit(solution)/shard_map/ppermute | solution.py:21
  24.7 1.8 copy.26
  27.8 2.5 copy.27
  30.3 81.9 %all-reduce.3.cloned.1.call-done = bf16[2,128,3072]{1,2,0:T(8,128)(2,1)} async-done(((bf16[2,128,3072]{1,2,0:T(8,128)(2,1)}), bf16[2,128,3072]{1,2,0:T(8,128)(2,1)}) %all-reduce.3.cloned.1.call-update) | async-done | bytes 1572880 | tf_op jit(solution)/shard_map/psum | solution.py:29
  112.2 3.8 %pad_maximum_fusion = bf16[2,384,3072]{1,2,0:T(8,128)(2,1)S(1)} fusion(bf16[2,128,3072]{1,2,0:T(8,128)(2,1)} %all-reduce.3.cloned.1.call-done, bf16[2,64,3072]{1,2,0:T(8,128)(2,1)} %copy.27, bf16[2,64,3072]{1,2,0:T(8,128)(2,1)S(1)} %copy.26, bf16[1,128,3072]{1,2,0:T(8,128)(2,1)S(1)} %copy.23, bf16[1,128,3072]{1,2,0:T(8,128)(2,1)S(1)} %copy.22), kind=kLoop, calls=%fused_computation.117 | loop fusion | flops 23592960 | bytes 9437184 | tf_op jit(solution)/shard_map/concatenate | solution.py:100
  116.0 2.7 fusion.98
  118.8 34.2 %while.44 = (s32[]{:T(128)}, f32[2,12,128]{2,1,0:T(8,128)}, s32[2]{0:T(128)}, bf16[2,128,12,128]{3,1,2,0:T(8,128)(2,1)}, bf16[2,384,12,128]{3,1,2,0:T(8,128)(2,1...) while((s32[]{:T(128)}, f32[2,12,128]{2,1,0:T(8,128)}, ...), condition=%wide.region_9.10_spmd.clone, body=%wide.region_1.9_spmd.clone.sunk | while | flops 164959488 | bytes 33304724 | solution.py:82
  120.0 1.9 constant_dynamic-slice_fusion.9
  125.7 2.6 convert_reduce_fusion.17
  130.0 2.0 copy.68
  132.0 2.9 bitcast_dynamic-update-slice_fusion.15
  137.1 1.9 constant_dynamic-slice_fusion.9
  142.8 2.6 convert_reduce_fusion.17
  147.0 2.0 copy.68
  149.1 2.9 bitcast_dynamic-update-slice_fusion.15
  153.7 58.3 %psum.36 = f32[3072]{0:T(1024)S(1)} all-reduce(f32[3072]{0:T(1024)S(1)} %reshape.126), channel_id=1, replica_groups=mesh['fsdp'=2,'tok'=16] {'tok'}, use_global_device_ids=true, to_apply=%region_10.11 | all-reduce | flops 3072 | bytes 24576 | tf_op jit(solution)/shard_map/psum | solution.py:115
  212.0 6.9 %fusion.103 = f32[1,1000]{1,0:T(1,128)S(1)} fusion(f32[3072,1]{0,1:T(1,128)S(1)} %bitcast.114, bf16[3072,1000]{0,1:T(8,128)(2,1)} %all-gather.2.cloned.1.call-done), kind=kOutput, calls=%fused_computation.140 | convolution fusion | flops 36864000 | bytes 6160288 | tf_op jit(solution)/shard_map/dot_general | solution.py:117
  222.0 4.9 %psum.37 = f32[1000]{0:T(1024)S(1)} all-reduce(f32[1000]{0:T(1024)S(1)} %fusion.95), channel_id=1, replica_groups=mesh['fsdp'=2,'tok'=16] {'fsdp'}, use_global_device_ids=true, to_apply=%region_13.14 | all-reduce | flops 1000 | bytes 8000 | tf_op jit(solution)/shard_map/psum | solution.py:119
  227.0 2.0 multiply_reduce_fusion.1
  228.9 1.9 subtract_multiply_fusion
  230.8 5.5 %fusion.104 = f32[1,3072]{1,0:T(1,128)S(1)} fusion(f32[1000,1]{0,1:T(1,128)S(1)} %bitcast.116, bf16[3072,1000]{0,1:T(8,128)(2,1)} %all-gather.2.cloned.1.call-done), kind=kOutput, calls=%fused_computation.141 | convolution fusion | flops 36864000 | bytes 6160288 | tf_op jit(solution)/shard_map/dot_general | solution.py:123
  236.4 42.7 %while.43 = (s32[]{:T(128)}, f32[24,128]{1,0:T(8,128)S(1)}, f32[24,128]{1,0:T(8,128)S(1)}, s32[2]{0:T(128)S(1)}, bf16[2,128,12,128]{3,1,2,0:T(8,128)(2,1)}, /*in...) while((s32[]{:T(128)}, f32[24,128]{1,0:T(8,128)S(1)}, ...), condition=%wide.region_28.29_spmd, body=%wide.region_16.28_spmd.sunk | while | flops 497625600 | bytes 43781616 | solution.py:82
  241.5 2.0 fusion.135
  245.4 1.7 convert_reduce_fusion.14
  247.2 3.7 %fusion.140 = f32[12,128]{1,0:T(8,128)S(1)} fusion(pred[12,128,384]{2,1,0:T(32,128)(4,1)S(1)} %get-tuple-element.762, f32[12,128]{1,0:T(8,128)S(1)} %negate_divide_fusion.2, pred[384]{0:T(512)(128)(4,1)S(1)} %get-tuple-element.754, bf16[128,12,128]{2,0,1:T(8,128)(2,1)S(1)} %dynamic-slice_bitcast_fusion.12, ...), kind=kOutput, calls=%fused_computation.27.clone.1 | convolution fusion | flops 161217024 | bytes 4626816 | tf_op jit(solution)/shard_map/transpose(jvp())/while/body/eval_jaxpr/checkpoint/qhd,khd->hqk/dot_general | solution.py:43
  250.9 3.9 %fusion.139 = f32[12,128]{1,0:T(8,128)S(1)} fusion(bf16[384,12,128]{2,0,1:T(8,128)(2,1)S(1)} %dynamic-slice_bitcast_fusion.13, f32[384,12]{0,1:T(8,128)S(1)} %add_rsqrt_fusion.8, f32[384,12]{0,1:T(8,128)S(1)} %broadcast_multiply_fusion.10, pred[12,128,384]{2,1,0:T(32,128)(4,1)S(1)} %get-tuple-element.762, f32[12,128]{1,0:T(8,128)S(1)} %negate_divide_fusion.2, ...), kind=kOutput, calls=%fused_computation.10.clone.1 | convolution fusion | flops 162003456 | bytes 4626816 | tf_op jit(solution)/shard_map/transpose(jvp())/while/body/eval_jaxpr/checkpoint/qhd,khd->hqk/dot_general | solution.py:43
  262.9 2.0 fusion.135
  266.8 1.7 convert_reduce_fusion.14
  268.5 3.7 %fusion.140 = f32[12,128]{1,0:T(8,128)S(1)} fusion(pred[12,128,384]{2,1,0:T(32,128)(4,1)S(1)} %get-tuple-element.762, f32[12,128]{1,0:T(8,128)S(1)} %negate_divide_fusion.2, pred[384]{0:T(512)(128)(4,1)S(1)} %get-tuple-element.754, bf16[128,12,128]{2,0,1:T(8,128)(2,1)S(1)} %dynamic-slice_bitcast_fusion.12, ...), kind=kOutput, calls=%fused_computation.27.clone.1 | convolution fusion | flops 161217024 | bytes 4626816 | tf_op jit(solution)/shard_map/transpose(jvp())/while/body/eval_jaxpr/checkpoint/qhd,khd->hqk/dot_general | solution.py:43
  272.3 3.9 %fusion.139 = f32[12,128]{1,0:T(8,128)S(1)} fusion(bf16[384,12,128]{2,0,1:T(8,128)(2,1)S(1)} %dynamic-slice_bitcast_fusion.13, f32[384,12]{0,1:T(8,128)S(1)} %add_rsqrt_fusion.8, f32[384,12]{0,1:T(8,128)S(1)} %broadcast_multiply_fusion.10, pred[12,128,384]{2,1,0:T(32,128)(4,1)S(1)} %get-tuple-element.762, f32[12,128]{1,0:T(8,128)S(1)} %negate_divide_fusion.2, ...), kind=kOutput, calls=%fused_computation.10.clone.1 | convolution fusion | flops 162003456 | bytes 4626816 | tf_op jit(solution)/shard_map/transpose(jvp())/while/body/eval_jaxpr/checkpoint/qhd,khd->hqk/dot_general | solution.py:43
  279.8 37.5 %all-reduce = (f32[3072]{0:T(1024)}, f32[3072]{0:T(1024)}) all-reduce(f32[3072]{0:T(1024)S(1)} %bitcast.105, f32[3072]{0:T(1024)S(1)} %bitcast.106), channel_id=1, replica_groups=mesh['fsdp'=2,'tok'=16] {'fsdp','tok'}, use_global_device_ids=true, to_apply=%region_29.30 | all-reduce | flops 6144 | bytes 49152 | tf_op jit(solution)/shard_map/psum | solution.py:125
  (197 shorter events, 48.5 us)
Async XLA Ops:
  8.0 104.2 %all-reduce.3.cloned.1.call-start = ((), (), s32[]{:S(2)}) async-start(), calls=%async_computation | async-start | bytes 3145728 | tf_op jit(solution)/shard_map/psum | solution.py:29
  13.1 198.9 %all-gather.2.cloned.1.call-start = ((), (), s32[]{:S(2)}) async-start(), calls=%async_computation.1 | async-start | bytes 9216000 | tf_op jit(solution)/shard_map/all_gather | solution.py:116
  17.2 7.5 %collective-permute-start = (bf16[2,64,3072]{2,1,0:T(8,128)(2,1)}, bf16[2,64,3072]{2,1,0:T(8,128)(2,1)}, u32[]{:S(2)}, u32[]{:S(2)}) collective-permute-start(bf16[2,64,3072]{2,1,0:T(8,128)(2,1)} %copy.24), channel_id=1, source_target_pairs={{0,1},{1,2},{2,3},{3,4},{4,5},{5,6},{6,7},{7,8},{8,9},{9,10},{10,1... | collective-permute-start | bytes 2359304 | tf_op jit(solution)/shard_map/ppermute | solution.py:21
  21.9 5.9 %collective-permute-start.1 = (bf16[2,64,3072]{2,1,0:T(8,128)(2,1)}, bf16[2,64,3072]{2,1,0:T(8,128)(2,1)}, u32[]{:S(2)}, u32[]{:S(2)}) collective-permute-start(bf16[2,64,3072]{2,1,0:T(8,128)(2,1)} %copy.25), channel_id=1, source_target_pairs={{1,0},{2,1},{3,2},{4,3},{5,4},{6,5},{7,6},{8,7},{9,8},{10,9},{11,1... | collective-permute-start | bytes 2359304 | tf_op jit(solution)/shard_map/ppermute | solution.py:22
  116.0 2.8 copy-start.7
  122.7 1.9 copy-start.2
  122.7 2.9 copy-start.8
  122.7 2.9 copy-start.9
  122.8 2.9 copy-start.12
  125.7 2.6 copy-start.10
  125.7 2.6 copy-start.13
  125.7 3.1 copy-start.15
  128.8 3.2 copy-start.16
  130.0 4.9 %copy-start.3 = (bf16[2,128,12,128]{3,1,2,0:T(8,128)(2,1)S(1)}, bf16[2,128,12,128]{3,1,2,0:T(8,128)(2,1)}, u32[]{:S(2)}) copy-start(bf16[2,128,12,128]{3,1,2,0:T(8,128)(2,1)} %get-tuple-element.810) | copy-start | bytes 2359300 | tf_op jit(solution)/shard_map/jvp()/while
  132.0 3.0 copy-start.19
  132.0 3.8 %copy-start.18 = (s32[2]{0:T(128)S(1)}, s32[2]{0:T(128)}, u32[]{:S(2)}) copy-start(s32[2]{0:T(128)} %copy-done.17) | copy-start | bytes 28 | tf_op jit(solution)/shard_map/jvp()/while
  139.8 1.9 copy-start.2
  139.8 2.9 copy-start.8
  139.8 2.9 copy-start.9
  139.8 2.9 copy-start.12
  142.7 2.6 copy-start.10
  142.7 2.6 copy-start.13
  142.7 3.1 copy-start.15
  145.9 3.2 copy-start.16
  147.0 5.0 %copy-start.3 = (bf16[2,128,12,128]{3,1,2,0:T(8,128)(2,1)S(1)}, bf16[2,128,12,128]{3,1,2,0:T(8,128)(2,1)}, u32[]{:S(2)}) copy-start(bf16[2,128,12,128]{3,1,2,0:T(8,128)(2,1)} %get-tuple-element.810) | copy-start | bytes 2359300 | tf_op jit(solution)/shard_map/jvp()/while
  149.1 3.0 copy-start.19
  149.1 3.9 %copy-start.18 = (s32[2]{0:T(128)S(1)}, s32[2]{0:T(128)}, u32[]{:S(2)}) copy-start(s32[2]{0:T(128)} %copy-done.17) | copy-start | bytes 28 | tf_op jit(solution)/shard_map/jvp()/while
  230.8 5.6 %copy-start = (bf16[2,384,12,128]{3,2,1,0:T(8,128)(2,1)S(1)}, bf16[2,384,12,128]{3,2,1,0:T(8,128)(2,1)}, u32[]{:S(2)}) copy-start(bf16[2,384,12,128]{3,2,1,0:T(8,128)(2,1)} %get-tuple-element.851) | copy-start | bytes 7077892
  230.8 5.6 %copy-start.11 = (f32[2,12,128]{2,1,0:T(8,128)S(1)}, f32[2,12,128]{2,1,0:T(8,128)}, u32[]{:S(2)}) copy-start(f32[2,12,128]{2,1,0:T(8,128)} %get-tuple-element.852) | copy-start | bytes 36868
  230.8 5.6 %copy-start.14 = (f32[2,12,128]{2,1,0:T(8,128)S(1)}, f32[2,12,128]{2,1,0:T(8,128)}, u32[]{:S(2)}) copy-start(f32[2,12,128]{2,1,0:T(8,128)} %get-tuple-element.853) | copy-start | bytes 36868
  230.8 5.6 %copy-start.21 = (s32[2]{0:T(128)S(1)}, s32[2]{0:T(128)}, u32[]{:S(2)}) copy-start(s32[2]{0:T(128)} %get-tuple-element.848) | copy-start | bytes 28
  236.5 1.8 copy-start.5
  (10 other events, 12.5 us)
Sparse Core Ops, SparseCore 0:
  13.2 98.9 all-reduce.2
Sparse Core Ops, SparseCore 1:
  23.5 82.3 all-gather.1
where the time goes:
time: 328 us; the launch traced here: 326 us
  blocking collectives  101 us (31%)
  waiting for transfers between devices  83.2 us (25%)
  local copies, waits for them, and re-layouts  45.1 us (14%)
  matrix products  39 us (12%)
  other arithmetic  32.7 us (10%)
  between operations  18.1 us (6%)
  starting transfers between devices  4.76 us (1%)
    psum x1, waiting for transfers between devices, broadcast(): return lax.psum(block, axis)  81.9 us
    psum x1, blocking collectives, body(): pooled = lax.psum(band_total, 'tok') / view_tokens  58.3 us
    psum x1, blocking collectives, body(): query_grad, key_grad = lax.psum((query_grad, key_grad), ('fsdp', 'tok'))  37.5 us
    dot_general x6, matrix products, group_total(): jnp.einsum('qhd,khd->hqk', query_norm, key_norm, preferred_element_type=j...  19.3 us
    dynamic_update_slice x12, local copies, waits for them, and re-layouts, attend_sum(): lax.map(per_group, jnp.arange(head_count // group_size, dtype=jnp.int32))  8.42 us
    dynamic_slice x4, local copies, waits for them, and re-layouts, per_group(): lax.dynamic_slice_in_dim(value_heads, first_head, group_size, 1)  7.86 us
    reduce_sum x8, other arithmetic, normalize(): variance = jnp.mean(centred * centred, -1, keepdims=True)  7.75 us
    dot_general x1, matrix products, body(): logits = jnp.dot(pooled, weight, precision=lax.Precision.HIGHEST)  6.86 us
  transfers between devices with their start and end apart: 4, of which 2 were waited for; matrix products, arithmetic and copies ran while one was open for 15% of the time, Pallas kernels for 0%

commit v1 on v0

v1 whole, which is shorter than its diff:
```python
import functools

import jax
import jax.numpy as jnp
from jax import lax
from jax.experimental import pallas as pl
from jax.experimental.pallas import tpu as pltpu
from jax.sharding import Mesh, PartitionSpec as P

HEAD = 128
ROW = 64
GBLK = 128
GROUP = 4
PER = 6
STEP = 2
NEG = -1e30
SCALE = HEAD**-0.5
LOG2E = 1.4426950408889634
F32 = jnp.float32
BF16 = jnp.bfloat16
VMEM = pl.BlockSpec(memory_space=pltpu.VMEM)
SMEM = pl.BlockSpec(memory_space=pltpu.SMEM)
PARAMS = pltpu.CompilerParams(vmem_limit_bytes=16 * 1024 * 1024)
ALONE = pltpu.CompilerParams(vmem_limit_bytes=63 * 1024 * 1024)
HBM = pl.BlockSpec(memory_space=pltpu.HBM)

NN = (((1,), (0,)), ((), ()))
NT = (((1,), (1,)), ((), ()))

SHARES = (0, 2, 1, 3)


def dot(a, b, dims):
    return lax.dot_general(a, b, dims, preferred_element_type=F32)


def two(x):
    zero = jnp.zeros_like(x[0])
    return jnp.concatenate(
        [jnp.concatenate([x[0], zero], axis=1), jnp.concatenate([zero, x[1]], axis=1)], axis=0
    )


def centring():
    row = lax.broadcasted_iota(jnp.int32, (HEAD, HEAD), 0)
    col = lax.broadcasted_iota(jnp.int32, (HEAD, HEAD), 1)
    centre = ((row == col).astype(F32) - 1.0 / HEAD).astype(BF16)
    return two((centre, centre)), two(((row == col).astype(F32).astype(BF16),) * 2)


def unit_rows(x, centre):
    x = dot(x, centre, NN)
    parts = []
    for i in range(2):
        part = x[:, i * HEAD:(i + 1) * HEAD]
        variance = jnp.sum(part * part, axis=1, keepdims=True) * (1.0 / HEAD)
        parts.append(part * lax.rsqrt(variance + 1e-06))
    return jnp.concatenate(parts, axis=1)


def thirds(x):
    a = x.astype(BF16)
    rest = x - a.astype(F32)
    b = rest.astype(BF16)
    c = (rest - b.astype(F32)).astype(BF16)
    pad = jnp.zeros((13, x.shape[1]), BF16)
    return jnp.concatenate([a, b, c, pad], axis=0)


def two_heads(q, keys, values, gain_q, gain_k, edge):
    centre, eye = centring()
    tile = lambda x, t: x[t * HEAD:(t + 1) * HEAD]
    side = lambda x, i: x[:, i * HEAD:(i + 1) * HEAD]
    beside = lambda *parts: jnp.concatenate(parts, axis=1)
    below = lambda *parts: jnp.concatenate(parts, axis=0)
    qn, qnt, qns = [], [], []
    for t in range(GROUP):
        qn.append((unit_rows(tile(q, t), centre) * gain_q).astype(BF16))
        x = jnp.transpose(qn[t])
        qns.append(x)
        qnt.append(two((tile(x, 0), tile(x, 1))))
    kn = [(unit_rows(tile(keys, t), centre) * gain_k).astype(BF16) for t in range(GROUP + 2)]

    last = GROUP + 1
    attn = []
    for b in range(GROUP):
        scores = dot(below(kn[b], kn[b + 1], kn[last]), qnt[b], NN)
        if b == 0:
            scores = below(scores[:ROW] + edge[0], scores[ROW:])
        if b == GROUP - 1:
            at = 2 * HEAD
            scores = below(scores[:at - ROW], scores[at - ROW:at] + edge[1], scores[at:])
        top = jnp.max(scores, axis=0, keepdims=True)
        expo = jnp.exp2((scores - top) * (SCALE * LOG2E))
        attn.append((expo * (1.0 / jnp.sum(expo, axis=0, keepdims=True))).astype(BF16))

    knt = [jnp.transpose(x) for x in kn]
    vt = dot(eye, values, NT).astype(BF16)
    vt = [side(vt, t) for t in range(GROUP + 2)]
    zero = jnp.zeros((HEAD, HEAD), BF16)
    results = []
    for i in range(2):
        both = [below(tile(knt[t], i), tile(vt[t], i)) for t in range(GROUP + 2)]
        back = [None] * (GROUP + 2)
        outs, negs = [], []
        for b in range(0, GROUP, 2):
            one, other = side(attn[b], i), side(attn[b + 1], i)
            pair = below(
                beside(tile(one, 0), zero),
                beside(tile(one, 1), tile(other, 0)),
                beside(zero, tile(other, 1)),
                beside(tile(one, 2), tile(other, 2)),
            )
            made = dot(beside(both[b], both[b + 1], both[b + 2], both[last]), pair, NN)
            queries = below(side(qn[b], i), side(qn[b + 1], i))
            outs.append(made[HEAD:])
            negs.append(beside(tile(qns[b], i), tile(qns[b + 1], i)) * made[:HEAD].astype(BF16))
            moved = dot(pair, queries, NN)
            for n, t in enumerate((b, b + 1, b + 2, last)):
                piece = tile(moved, n)
                back[t] = piece if back[t] is None else back[t] + piece
        moved = [side(kn[t], i) * back[t].astype(BF16) for t in range(GROUP + 2)]
        jac = dot(beside(*[tile(v, i) for v in vt]), below(*moved), NN)
        jac = jac - dot(beside(*[o.astype(BF16) for o in outs]), beside(*negs), NT)
        sums = outs[0] + outs[1]
        sums = side(sums, 0) + side(sums, 1)
        results.append((jnp.sum(jnp.transpose(sums), axis=0, keepdims=True), jac))
    return results


def attend_kernel(count, place, gain_q, gain_k, q, k, v, near, far, kept, there, k_core, v_core,
                  first_kept, first_given, kv_last, q_core, q_row, part, part_there, logits, jac,
                  weight, qbuf, kbuf, vbuf, jbuf, pooled, sems, late, leave):
    mine, odd_layer, row, core, leading, here = (place[i] for i in (0, 1, 3, 4, 5, 6))
    edge = [jnp.where(place[i] == 1, NEG, 0.0) for i in (7, 8)]
    tokens = q.shape[0]
    width = STEP * HEAD
    steps = PER // STEP
    span = GROUP * tokens + 2 * ROW
    paired = pl.multiple_of((1 - odd_layer) * (span - ROW), ROW)
    other = pl.multiple_of(odd_layer * (span - ROW), ROW)

    def band(row, core, shift):
        return pl.ds(pl.multiple_of((row * 2 + core) * tokens + shift, ROW), tokens)

    def copies(step, kind, even=True):
        own = pl.ds(pl.multiple_of((mine * steps + step) * width, width), width)
        half = pl.ds(pl.multiple_of((row * steps + step) * width, width), width)
        cols = pl.ds(pl.multiple_of(step * width, width), width)
        if kind == 0:
            moves = [
                (q.at[:, own], band(row, core, 0)),
                (q_core.at[:, half], band(row, 1 - core, 0)),
                (q_row.at[0, :, cols], band(1 - row, core, 0)),
                (q_row.at[1, :, cols], band(1 - row, 1 - core, 0)),
            ]
        else:
            i = kind - 1
            raw, raw_core = ((k, k_core), (v, v_core))[i]
            first, shared = ((first_kept, kept), (first_given, there))[i if even else 1 - i]
            moves = [
                (raw.at[:, own], band(row, core, ROW)),
                (raw_core.at[:, half], band(row, 1 - core, ROW)),
                (kv_last.at[i, :, cols], band(1 - row, 1 - leading, ROW)),
                (near.at[i * ROW:(i + 1) * ROW, cols], pl.ds(paired, ROW)),
                (far.at[i * ROW:(i + 1) * ROW, cols], pl.ds(other, ROW)),
                (first.at[:, cols], band(1 - row, leading, ROW)),
                (shared.at[:, cols], pl.ds(span, GBLK)),
            ]
        buf = (qbuf, kbuf, vbuf)[kind]
        return [
            pltpu.make_async_copy(a, buf.at[step, b], sems.at[step, kind, n]) for n, (a, b) in enumerate(moves)
        ]

    def rows_of(readout):
        return pltpu.make_async_copy(readout, weight, late.at[0])

    def jacobian(step):
        heads = pl.ds(step * STEP, STEP)
        return pltpu.make_async_copy(jbuf.at[heads], jac.at[heads], leave.at[step])

    def start(step):
        for copy in copies(step, 0):
            copy.start()

        @pl.when(odd_layer == 0)
        def _():
            for copy in copies(step, 1, True) + copies(step, 2, True):
                copy.start()

        @pl.when(odd_layer == 1)
        def _():
            for copy in copies(step, 1, False) + copies(step, 2, False):
                copy.start()

    start(0)

    @pl.loop(0, steps)
    def _(step):
        @pl.when(step + 1 < steps)
        def _():
            start(step + 1)

        @pl.when((step == max(steps - 2, 0)) & (here == 1))
        def _():
            rows_of(part).start()

        @pl.when((step == max(steps - 2, 0)) & (here == 0))
        def _():
            rows_of(part_there).start()

        at = [pl.ds(mine * PER + step * STEP + i, 1) for i in range(STEP)]
        pair = [jnp.concatenate([gain[i, :] for i in at], axis=1) for gain in (gain_q, gain_k)]
        for copy in copies(step, 0) + copies(step, 1) + copies(step, 2):
            copy.wait()
        made = two_heads(qbuf[step], kbuf[step], vbuf[step], *pair, edge)
        for i in range(STEP):
            jbuf[step * STEP + i] = made[i][1]
        jacobian(step).start()
        pooled[pl.ds(step, 1), :] = jnp.concatenate([x for x, _ in made], axis=1)

    rows_of(part).wait()
    sums = jnp.concatenate([pooled[i:i + 1, :] for i in range(steps)], axis=1)
    made = dot(thirds(sums * (1.0 / count)), weight[...], NT)
    made = jnp.sum(made, axis=0, keepdims=True)
    made = jnp.concatenate([made, jnp.zeros((1, -made.shape[1] % HEAD), F32)], axis=1)
    made = jnp.concatenate([made[:, i:i + HEAD] for i in range(0, made.shape[1], HEAD)], axis=0)
    logits[...] = jnp.broadcast_to(made[None], logits.shape)
    for step in range(steps):
        jacobian(step).wait()


def attend(devices, count, place, gain_q, gain_k, q, k, v, near, far, kept, there, k_core, v_core, first_kept,
           first_given, kv_last, q_core, q_row, part, part_there):
    tokens = q.shape[0]
    keys = GROUP * tokens + 2 * ROW + GBLK
    width = STEP * HEAD
    steps = PER // STEP
    return pl.pallas_call(
        functools.partial(attend_kernel, count),
        out_shape=(
            jax.ShapeDtypeStruct((devices, -(-part.shape[0] // HEAD), HEAD), F32),
            jax.ShapeDtypeStruct((PER, HEAD, HEAD), F32),
        ),
        in_specs=[SMEM, VMEM, VMEM] + [HBM] * 16,
        out_specs=(VMEM, HBM),
        scratch_shapes=[
            pltpu.VMEM(part.shape, BF16),
            pltpu.VMEM((steps, GROUP * tokens, width), BF16),
            pltpu.VMEM((steps, keys, width), BF16),
            pltpu.VMEM((steps, keys, width), BF16),
            pltpu.VMEM((PER, HEAD, HEAD), F32),
            pltpu.VMEM((8, width), F32),
            pltpu.SemaphoreType.DMA((steps, 3, 7)),
            pltpu.SemaphoreType.DMA((1,)),
            pltpu.SemaphoreType.DMA((steps,)),
        ],
        compiler_params=ALONE,
        cost_estimate=pl.CostEstimate(flops=1_200_000_000, bytes_accessed=6_000_000, transcendentals=1_200_000),
        name="attend",
    )(place, gain_q, gain_k, q, k, v, near, far, kept, there, k_core, v_core, first_kept, first_given,
      kv_last, q_core, q_row, part, part_there)


def tail_kernel(count, classes, views, place, logits, part, part_there, jac, entropy, total, parts, weight, jbuf, sems):
    rows = weight.shape[0]
    pieces = [(i, min(HEAD, rows - i)) for i in range(0, rows, HEAD)]
    pieces = pieces[:-2] + [(pieces[-2][0], rows - pieces[-2][0])]

    def rows_of(readout):
        return [
            pltpu.make_async_copy(readout.at[pl.ds(i, n)], weight.at[pl.ds(i, n)], sems.at[j])
            for j, (i, n) in enumerate(pieces)
        ]

    gathered = pltpu.make_async_copy(logits, parts, sems.at[len(pieces) + 1])
    gathered.start()
    jacobian = pltpu.make_async_copy(jac, jbuf, sems.at[len(pieces)])
    jacobian.start()

    @pl.when(place[6] == 1)
    def _():
        for copy in rows_of(part):
            copy.start()

    @pl.when(place[6] == 0)
    def _():
        for copy in rows_of(part_there):
            copy.start()

    gathered.wait()
    per = parts.shape[0] // views
    tile = parts.shape[1:]
    index = lax.broadcasted_iota(jnp.int32, tile, 0) * HEAD + lax.broadcasted_iota(jnp.int32, tile, 1)
    valid = index < classes
    over_all = lambda f, x: f(f(x, axis=1, keepdims=True), axis=0, keepdims=True)
    mean = jnp.zeros(tile, F32)
    own = jnp.zeros(tile, F32)
    for i in range(views):
        x = jnp.where(valid, jnp.sum(parts[i * per:(i + 1) * per], axis=0), NEG)
        x = jnp.exp(x - over_all(jnp.max, x))
        x = x / over_all(jnp.sum, x)
        mean = mean + x
        own = jnp.where(place[2] == i, x, own)
    mean = mean * (1.0 / views)
    log = jnp.log(jnp.where(valid, mean, 1.0))
    entropy[...] = -over_all(jnp.sum, mean * log)
    upstream = (log + 1.0) * (-1.0 / views)
    dlogits = own * (upstream - over_all(jnp.sum, own * upstream))
    dlogits = jnp.concatenate([dlogits[i:i + 1] for i in range(tile[0])], axis=1)
    dlogits = thirds(dlogits)
    grad = jnp.zeros((dlogits.shape[0], weight.shape[1]), F32)
    for copy, (i, n) in zip(rows_of(part), pieces):
        copy.wait()
        grad = grad + dot(dlogits[:, i:i + n], weight[i:i + n, :], NN)
    grad = jnp.sum(grad, axis=0, keepdims=True) * (1.0 / count)
    jacobian.wait()
    rows = []
    for h in range(PER):
        g = thirds(grad[:, h * HEAD:(h + 1) * HEAD])
        j = jbuf[h]
        high = j.astype(BF16)
        low = (j - high.astype(F32)).astype(BF16)
        t = dot(g, high, NN) + dot(g, low, NN)
        rows.append(jnp.sum(t, axis=0, keepdims=True))
    rows.append(jnp.zeros((total.shape[0] - PER, HEAD), F32))
    total[...] = jnp.concatenate(rows, axis=0).astype(BF16)


def tail(count, classes, views, place, parts, part, part_there, jac):
    return pl.pallas_call(
        functools.partial(tail_kernel, count, classes, views),
        out_shape=(
            jax.ShapeDtypeStruct((1, 1), F32),
            jax.ShapeDtypeStruct((8, HEAD), BF16),
        ),
        in_specs=[SMEM] + [HBM] * 4,
        out_specs=(VMEM, VMEM),
        scratch_shapes=[
            pltpu.VMEM(parts.shape, F32),
            pltpu.VMEM(part.shape, BF16),
            pltpu.VMEM(jac.shape, F32),
            pltpu.SemaphoreType.DMA((-(-part.shape[0] // HEAD) + 1,)),
        ],
        compiler_params=ALONE,
        name="tail",
    )(place, parts, part, part_there, jac)


def finish_kernel(parts, gain_q, gain_k, q_grad, k_grad):
    for member in range(GROUP):
        total = parts[member].astype(F32)
        for i in range(member + GROUP, parts.shape[0], GROUP):
            total = total + parts[i].astype(F32)
        total = total[:PER] * SCALE
        at = slice(SHARES[member] * PER, (SHARES[member] + 1) * PER)
        q_grad[at, :] = total / gain_q[at, :]
        k_grad[at, :] = total / gain_k[at, :]


def finish(parts, gain_q, gain_k):
    shape = jax.ShapeDtypeStruct(gain_q.shape, F32)
    return pl.pallas_call(
        finish_kernel,
        out_shape=(shape, shape),
        in_specs=[VMEM] * 3,
        out_specs=(VMEM, VMEM),
        compiler_params=PARAMS,
        name="finish",
    )(parts, gain_q, gain_k)


def group_readout(readout, mine, group_rows):
    views = lax.axis_size("fsdp")
    layers = lax.axis_size("layer")
    rows = readout.shape[0]

    def cut(x, first):
        part = lax.dynamic_slice_in_dim(x, first * group_rows, group_rows, 0).T
        return lax.optimization_barrier(part)

    if views == 2 and rows % group_rows == 0:
        per = rows // group_rows
        part = cut(readout, mine % per)
        pairs = []
        for t in range(layers * GROUP):
            f = SHARES[t % GROUP] // per
            pairs.append((f * layers * GROUP + t, (1 - f) * layers * GROUP + t))
        there = lax.ppermute(part, ("fsdp", "layer", "row", "core"), pairs)
        return part, there, (lax.axis_index("fsdp") == mine // per).astype(jnp.int32)
    part = cut(lax.all_gather(readout, "fsdp", axis=0, tiled=True), mine)
    return part, part, jnp.int32(1)


def xor_layer(x, bit):
    return lax.ppermute(x, "layer", [(i, i ^ bit) for i in range(lax.axis_size("layer"))])


def other_core(x):
    return lax.ppermute(x, "core", [(0, 1), (1, 0)])


def other_row(x):
    return lax.ppermute(x, "row", [(0, 1), (1, 0)])


def every_device(x):
    return lax.all_to_all(x, ("fsdp", "layer", "row", "core"), 0, 0, tiled=True)


def after(x, *earlier):
    return lax.optimization_barrier((x, earlier))[0]


def body(queries, keys, values, readout, global_block, q_gain, k_gain):
    views = lax.axis_size("fsdp")
    layers = lax.axis_size("layer")
    core = lax.axis_index("core")
    row = lax.axis_index("row")
    mine = core * 2 + row
    theirs = core * 2 + 1 - row
    layer = lax.axis_index("layer")
    odd_layer = layer & 1
    q, k, v = queries[0], keys[0], values[0]
    tokens, channels = q.shape
    wide = channels // GROUP
    classes = readout.shape[1]
    count = tokens * layers * GROUP

    def columns(x, share):
        return lax.dynamic_slice_in_dim(x, share * wide, wide, 1)

    def kv_columns(share):
        return jnp.stack([columns(k, share), columns(v, share)])

    owner = global_block[0] // (tokens // GBLK)
    home = owner // GROUP
    leading = owner & 1
    leads = leading == core

    def half(x):
        return lax.dynamic_slice_in_dim(x, (1 - core) * 2 * wide, 2 * wide, 1)

    k_core, v_core = (other_core(x) for x in lax.optimization_barrier((half(k), half(v))))
    kv_core = jnp.stack([k_core, v_core])
    own = jnp.stack([columns(k, mine), columns(v, mine)])
    own_theirs = jnp.stack([columns(k, theirs), columns(v, theirs)])
    core_mine = lax.dynamic_slice_in_dim(kv_core, row * wide, wide, 2)
    core_theirs = lax.dynamic_slice_in_dim(kv_core, (1 - row) * wide, wide, 2)
    lead = jnp.where(leads, own_theirs, core_theirs)
    first_given = other_row(jnp.where(odd_layer == 0, lead[1], lead[0]))
    first_kept = other_row(jnp.where(odd_layer == 0, lead[0], lead[1]))
    kv_last = other_row(jnp.where(leads, core_theirs, own_theirs))
    part, part_there, here = group_readout(after(readout, v_core), mine, wide)
    place = jnp.stack([jnp.int32(x) for x in (mine, odd_layer, lax.axis_index("fsdp"), row, core, leading, here, layer == 0, layer == layers - 1)])
    outer = []
    for z in range(layers):
        other = z + 1 if z % 2 else z - 1
        if 0 <= other < layers:
            outer.append((z, other))

    near_row = (owner >> 1) & 1 == row
    held = jnp.where(leads, own, core_mine)
    given = jnp.where(near_row, jnp.where(odd_layer == 0, held[1], held[0]), first_given)
    kept = jnp.where(near_row, jnp.where(odd_layer == 0, held[0], held[1]), first_kept)
    given = xor_layer(given, 1)
    kept = jnp.where(layer == home, kept, given)
    kv_last = after(kv_last, kept)

    def band(index, rows):
        at_row, at_core = index >> 1, index & 1
        near = jnp.where(at_core == core, own[:, rows], core_mine[:, rows])
        keys = jnp.where(odd_layer == 0, first_kept[rows], first_given[rows])
        values = jnp.where(odd_layer == 0, first_given[rows], first_kept[rows])
        far_row = jnp.where(at_core == leading, jnp.stack([keys, values]), kv_last[:, rows])
        return jnp.where(at_row == row, near, far_row).reshape(2 * ROW, -1)

    first = band(0, slice(0, ROW))
    final = band(GROUP - 1, slice(tokens - ROW, tokens))
    near = xor_layer(jnp.where(odd_layer == 0, final, first), 1)
    far = lax.ppermute(jnp.where(odd_layer == 0, first, final), "layer", outer)
    part_there = after(part_there, near)
    q_late = after(q, first_given)
    q_core = other_core(half(after(q, v_core)))
    q_row = jnp.stack([columns(q_late, theirs), lax.dynamic_slice_in_dim(q_core, (1 - row) * wide, wide, 1)])
    q_row = other_row(q_row)
    bit = 2
    while bit < layers:
        kept = jnp.where(layer // bit == home // bit, kept, xor_layer(kept, bit))
        bit *= 2
    there = xor_layer(kept, 1)

    gain_q, gain_k = q_gain.reshape(-1, HEAD), k_gain.reshape(-1, HEAD)
    devices = views * layers * GROUP
    logits, jac = attend(
        devices, count, place, gain_q, gain_k, q, k, v, near, far, kept, there, k_core, v_core, first_kept,
        first_given, kv_last, q_core, q_row, part, part_there,
    )
    parts = every_device(logits)
    entropy, total = tail(count, classes, views, place, parts, part, part_there, jac)
    total = jnp.broadcast_to(total, (devices,) + total.shape)
    q_grad, k_grad = finish(every_device(total), gain_q, gain_k)
    return (entropy[0, 0], q_grad.reshape(-1), k_grad.reshape(-1))


def solution(mesh):
    views, toks = mesh.devices.shape
    grouped = Mesh(
        mesh.devices.reshape(views, toks // GROUP, GROUP // 2, 2), ("fsdp", "layer", "row", "core")
    )
    tok = ("layer", "row", "core")
    in_specs = (
        P("fsdp", tok, None),
        P("fsdp", tok, None),
        P("fsdp", tok, None),
        P("fsdp", None),
        P("fsdp"),
        P(),
        P(),
    )
    out_specs = (P(), P(), P())
    return jax.shard_map(body, mesh=grouped, in_specs=in_specs, out_specs=out_specs, check_vma=False)
```

time: 328 us -> 76.8 us (0.23)
  blocking collectives: 101 us -> 23 us
  waiting for transfers between devices: 83.2 us -> 8.12 us
  local copies, waits for them, and re-layouts: 45.1 us -> 4.43 us
  matrix products: 39 us -> 0 us
  other arithmetic: 32.7 us -> 2.18 us
  starting transfers between devices: 4.76 us -> 22.9 us
  between operations: 18.1 us -> 1.57 us
  Pallas kernels: 0 us -> 14.1 us
    psum x3 -> x0, blocking collectives: 101 us -> none  [the longest x1 58.3 us: body(): pooled = lax.psum(band_total, 'tok') / view_tokens]
    psum x1 -> x0, waiting for transfers between devices: 81.9 us -> none  [broadcast(): return lax.psum(block, axis)]
    dot_general x12 -> x0, matrix products: 33.8 us -> none  [the longest x6 19.3 us: group_total(): jnp.einsum('qhd,khd->hqk', query_norm, key_norm, preferred_element_type=j...]
    all_to_all x0 -> x2, blocking collectives: none -> 23 us  [every_device(): return lax.all_to_all(x, ('fsdp', 'layer', 'row', 'core'), 0, 0, tiled=True)]
    reduce_sum x24 -> x0, other arithmetic: 20.5 us -> none  [the longest x8 7.75 us: normalize(): variance = jnp.mean(centred * centred, -1, keepdims=True)]
    ppermute x2 -> x13, starting transfers between devices: 4.68 us -> 22.9 us  [the longest x4 10.8 us: xor_layer(): lax.ppermute(x, 'layer', [(i, i ^ bit) for i in range(lax.axis_size('laye...]
    pallas_call x0 -> x3, Pallas kernels: none -> 14.1 us  [the longest x1 9.99 us: attend(): pl.pallas_call(functools.partial(attend_kernel, count), out_shape=(jax.Sh...]
    dynamic_slice x14 -> x3, local copies, waits for them, and re-layouts: 12.3 us -> 1.4 us  [the longest x2 1.31 us: half(): return lax.dynamic_slice_in_dim(x, (1 - core) * 2 * wide, 2 * wide, 1)]
  transfers between devices with their start and end apart: 4 -> 13, of which waited for: 2 -> 6; matrix products, arithmetic and copies ran while one was open for 15% -> 4% of each run, Pallas kernels for 0% -> 0%
where the time goes in v1:
time: 76.8 us; the launch traced here: 76.3 us
  blocking collectives  23 us (30%)
  starting transfers between devices  22.9 us (30%)
  Pallas kernels  14.1 us (18%)
  waiting for transfers between devices  8.12 us (11%)
  local copies, waits for them, and re-layouts  4.43 us (6%)
  other arithmetic  2.18 us (3%)
  between operations  1.57 us (2%)
    all_to_all x2, blocking collectives, every_device(): return lax.all_to_all(x, ('fsdp', 'layer', 'row', 'core'), 0, 0, tiled=True)  23 us
    ppermute x4, starting transfers between devices, xor_layer(): lax.ppermute(x, 'layer', [(i, i ^ bit) for i in range(lax.axis_size('laye...  10.8 us
    pallas_call x1, Pallas kernels, attend(): pl.pallas_call(functools.partial(attend_kernel, count), out_shape=(jax.Sh...  9.99 us
    ppermute x4, starting transfers between devices, other_row(): return lax.ppermute(x, 'row', [(0, 1), (1, 0)])  6.56 us
    ppermute x4, waiting for transfers between devices, xor_layer(): lax.ppermute(x, 'layer', [(i, i ^ bit) for i in range(lax.axis_size('laye...  3.91 us
    ppermute x1, starting transfers between devices, group_readout(): there = lax.ppermute(part, ('fsdp', 'layer', 'row', 'core'), pairs)  3.49 us
    pallas_call x1, Pallas kernels, tail(): pl.pallas_call(functools.partial(tail_kernel, count, classes, views), out...  3.47 us
    ppermute x4, waiting for transfers between devices, other_row(): return lax.ppermute(x, 'row', [(0, 1), (1, 0)])  3.2 us
  transfers between devices with their start and end apart: 13, of which 6 were waited for; matrix products, arithmetic and copies ran while one was open for 4% of the time, Pallas kernels for 0%

profile of v1, /device:TPU:0, one launch (start us, length us, event | category | flops | bytes accessed | tf_op | source)
XLA Modules:
  0.0 76.3 jit_solution(8305041336814418572)
XLA Ops:
  0.7 1.3 %dynamic-slice_bitcast_fusion.1 = (bf16[128,1536]{1,0:T(8,128)(2,1)S(1)}, bf16[128,1536]{1,0:T(8,128)(2,1)S(1)}) fusion(bf16[1,128,3072]{2,1,0:T(8,128)(2,1)} %param.9, s32[]{:T(128)S(6)} %select_n.194, bf16[1,128,3072]{2,1,0:T(8,128)(2,1)} %param.8), kind=kLoop, calls=%fused_computation.15 | loop fusion | bytes 1572868 | tf_op jit(solution)/shard_map/dynamic_slice | solution.py:442
  1.9 0.5 collective-permute-start.1
  3.4 0.4 collective-permute-done.1.v_core
  3.8 0.6 collective-permute-done.k_core
  4.4 0.3 fusion
  4.7 0.4 copy-done.10
  5.1 3.0 %collective-permute-start.3 = (bf16[128,768]{1,0:T(8,128)(2,1)S(1)}, bf16[128,768]{1,0:T(8,128)(2,1)S(1)}, u32[]{:S(2)}, u32[]{:S(2)}) collective-permute-start(bf16[128,768]{1,0:T(8,128)(2,1)S(1)} %get-tuple-element.47), channel_id=1, source_target_pairs={{0,2},{2,0},{1,3},{3,1},{4,6},{6,4},{5,7},{7,5},{8,10},{10,8},{9,1... | collective-permute-start | bytes 589832 | tf_op jit(solution)/shard_map/ppermute | solution.py:404
  8.2 0.6 collective-permute-start.2
  8.8 1.5 %collective-permute-start.4 = (bf16[2,128,768]{2,1,0:T(8,128)(2,1)S(1)}, bf16[2,128,768]{2,1,0:T(8,128)(2,1)S(1)}, u32[]{:S(2)}, u32[]{:S(2)}) collective-permute-start(bf16[2,128,768]{2,1,0:T(8,128)(2,1)S(1)} %get-tuple-element.36), channel_id=1, source_target_pairs={{0,2},{2,0},{1,3},{3,1},{4,6},{6,4},{5,7},{7,5},{8,10},{10,8},{9,1... | collective-permute-start | bytes 1179656 | tf_op jit(solution)/shard_map/ppermute | solution.py:404
  10.3 0.1 dynamic-slice_bitcast_fusion.part
  10.4 3.5 %collective-permute-start.12 = (bf16[1000,768]{1,0:T(8,128)(2,1)S(1)}, bf16[1000,768]{1,0:T(8,128)(2,1)S(1)}, u32[]{:S(2)}, u32[]{:S(2)}) collective-permute-start(bf16[1000,768]{1,0:T(8,128)(2,1)S(1)} %dynamic-slice_bitcast_fusion.part), channel_id=1, source_target_pairs={{0,16},{17,1},{2,18},{19,3},{4,20},{21,5},{6,22},{23,7},{8,24},{25... | collective-permute-start | bytes 4608008 | tf_op jit(solution)/shard_map/ppermute | solution.py:389
  14.0 2.0 %collective-permute-start.5 = (bf16[128,768]{1,0:T(8,128)(2,1)S(1)}, bf16[128,768]{1,0:T(8,128)(2,1)S(1)}, u32[]{:S(2)}, u32[]{:S(2)}) collective-permute-start(bf16[128,768]{1,0:T(8,128)(2,1)S(1)} %bitcast_select_fusion), channel_id=1, source_target_pairs={{0,4},{4,0},{8,12},{12,8},{1,5},{5,1},{9,13},{13,9},{2,6},{6,2},{1... | collective-permute-start | bytes 589832 | tf_op jit(solution)/shard_map/ppermute | solution.py:396
  16.0 2.0 %collective-permute-done.2.first_kept = bf16[128,768]{1,0:T(8,128)(2,1)S(1)} collective-permute-done((bf16[128,768]{1,0:T(8,128)(2,1)S(1)}, bf16[128,768]{1,0:T(8,128)(2,1)S(1)}, u32[]{:S(2)}, u32[]{:S(2)}) %collective-permute-start.2) | collective-permute-done | bytes 196640 | tf_op jit(solution)/shard_map/ppermute | solution.py:404
  18.1 1.8 %collective-permute-done.5 = bf16[128,768]{1,0:T(8,128)(2,1)S(1)} collective-permute-done((bf16[128,768]{1,0:T(8,128)(2,1)S(1)}, bf16[128,768]{1,0:T(8,128)(2,1)S(1)}, u32[]{:S(2)}, u32[]{:S(2)}) %collective-permute-start.5) | collective-permute-done | bytes 196640 | tf_op jit(solution)/shard_map/ppermute | solution.py:396
  19.9 2.9 %collective-permute-start.8 = (bf16[128,768]{1,0:T(8,128)(2,1)S(1)}, bf16[128,768]{1,0:T(8,128)(2,1)S(1)}, u32[]{:S(2)}, u32[]{:S(2)}) collective-permute-start(bf16[128,768]{1,0:T(8,128)(2,1)S(1)} %fusion.9), channel_id=1, source_target_pairs={{0,8},{4,12},{8,0},{12,4},{1,9},{5,13},{9,1},{13,5},{2,10},{6,14},... | collective-permute-start | bytes 589832 | tf_op jit(solution)/shard_map/ppermute | solution.py:396
  22.9 0.9 %pad_maximum_fusion.2 = bf16[2,128,768]{2,1,0:T(8,128)(2,1)} fusion(bf16[1,128,768]{2,1,0:T(8,128)(2,1)S(1)} %dynamic-slice_bitcast_fusion.3, bf16[1,128,768]{2,1,0:T(8,128)(2,1)S(1)} %dynamic-slice_bitcast_fusion.4), kind=kLoop, calls=%fused_computation.14 | loop fusion | flops 196608 | bytes 786432 | tf_op jit(solution)/shard_map/stack | solution.py:485
  23.7 1.5 %collective-permute-start.11 = (bf16[2,128,768]{2,1,0:T(8,128)(2,1)}, bf16[2,128,768]{2,1,0:T(8,128)(2,1)}, u32[]{:S(2)}, u32[]{:S(2)}) collective-permute-start(bf16[2,128,768]{2,1,0:T(8,128)(2,1)} %pad_maximum_fusion.2), channel_id=1, source_target_pairs={{0,2},{2,0},{1,3},{3,1},{4,6},{6,4},{5,7},{7,5},{8,10},{10,8},{9,1... | collective-permute-start | bytes 1179656 | tf_op jit(solution)/shard_map/ppermute | solution.py:404
  25.2 1.2 %collective-permute-done.4.kv_last = bf16[2,128,768]{2,1,0:T(8,128)(2,1)S(1)} collective-permute-done((bf16[2,128,768]{2,1,0:T(8,128)(2,1)S(1)}, bf16[2,128,768]{2,1,0:T(8,128)(2,1)S(1)}, u32[]{:S(2)}, u32[]{:S(2)}) %collective-permute-start.4) | collective-permute-done | bytes 393248 | tf_op jit(solution)/shard_map/ppermute | solution.py:404
  26.4 0.1 broadcast_select_fusion.3
  26.6 0.7 broadcast_select_fusion.4
  27.3 2.1 %collective-permute-start.6 = (bf16[128,768]{1,0:T(8,128)(2,1)}, bf16[128,768]{1,0:T(8,128)(2,1)}, u32[]{:S(2)}, u32[]{:S(2)}) collective-permute-start(bf16[128,768]{1,0:T(8,128)(2,1)} %bitcast.27), channel_id=1, source_target_pairs={{0,4},{4,0},{8,12},{12,8},{1,5},{5,1},{9,13},{13,9},{2,6},{6,2},{1... | collective-permute-start | bytes 589832 | tf_op jit(solution)/shard_map/ppermute | solution.py:396
  29.4 1.3 %collective-permute-start.7 = (bf16[128,768]{1,0:T(8,128)(2,1)S(1)}, bf16[128,768]{1,0:T(8,128)(2,1)}, u32[]{:S(2)}, u32[]{:S(2)}) collective-permute-start(bf16[128,768]{1,0:T(8,128)(2,1)S(1)} %bitcast.67), channel_id=1, source_target_pairs={{4,8},{8,4},{5,9},{9,5},{6,10},{10,6},{7,11},{11,7},{20,24},{24,20... | collective-permute-start | bytes 589832 | tf_op jit(solution)/shard_map/ppermute | solution.py:481
  30.8 3.8 %collective-permute-start.9 = (bf16[128,768]{1,0:T(8,128)(2,1)S(1)}, bf16[128,768]{1,0:T(8,128)(2,1)}, u32[]{:S(2)}, u32[]{:S(2)}) collective-permute-start(bf16[128,768]{1,0:T(8,128)(2,1)S(1)} %broadcast_select_fusion.2.kept), channel_id=1, source_target_pairs={{0,4},{4,0},{8,12},{12,8},{1,5},{5,1},{9,13},{13,9},{2,6},{6,2},{1... | collective-permute-start | bytes 589832 | tf_op jit(solution)/shard_map/ppermute | solution.py:396
  34.6 0.6 stack.97.place
  35.2 1.1 %copy-done.3 = bf16[1000,768]{1,0:T(8,128)(2,1)} copy-done((bf16[1000,768]{1,0:T(8,128)(2,1)}, bf16[1000,768]{1,0:T(8,128)(2,1)S(1)}, u32[]{:S(2)}) %copy-start.3) | copy-done | bytes 1536024
  36.3 2.1 %collective-permute-done.9.there = bf16[128,768]{1,0:T(8,128)(2,1)} collective-permute-done((bf16[128,768]{1,0:T(8,128)(2,1)S(1)}, bf16[128,768]{1,0:T(8,128)(2,1)}, u32[]{:S(2)}, u32[]{:S(2)}) %collective-permute-start.9) | collective-permute-done | bytes 196640 | tf_op jit(solution)/shard_map/ppermute | solution.py:396
  38.5 10.0 %attend.1 = (f32[32,8,128]{2,1,0:T(8,128)}, f32[6,128,128]{2,1,0:T(8,128)}) custom-call(s32[9]{0:T(128)} %stack.97.place, f32[24,128]{1,0:T(8,128)} %bitcast.56, f32[24,128]{1,0:T(8,128)} %bitcast.58, bf16[128,3072]{1,0:T(8,128)(2,1)} %bitcast.62, bf16[128,3072]{1,0:T(8,128)(2,1)} %bitcast.60, bf16[128,3072]{1,0:T(8,128)(2,1)} %bitcast.61, ...), custom_call_target="tpu_custom_call" | custom-call | flops 1200000000 | bytes 6000000 | tf_op jit(solution)/shard_map/attend/pallas_call | solution.py:239
  48.5 13.9 %all_to_all.10.logits = f32[32,8,128]{2,1,0:T(8,128)} all-to-all(f32[32,8,128]{2,1,0:T(8,128)} %get-tuple-element.23), channel_id=1, replica_groups=mesh['fsdp'=2,'layer'=4,'row'=2,'core'=2] {'fsdp','layer','row','core'}, dimensions={0} | all-to-all | bytes 262144 | tf_op jit(solution)/shard_map/all_to_all | solution.py:408
  62.4 3.5 %tail.1 = (f32[1,1]{1,0:T(1,128)}, bf16[8,128]{1,0:T(8,128)(2,1)}) custom-call(s32[9]{0:T(128)} %stack.97.place, f32[32,8,128]{2,1,0:T(8,128)} %all_to_all.10.logits, bf16[1000,768]{1,0:T(8,128)(2,1)} %copy-done.2, bf16[1000,768]{1,0:T(8,128)(2,1)} %copy-done.3, f32[6,128,128]{2,1,0:T(8,128)} %get-tuple-element.24.jac), custom_call_target="tpu_custom_call" | custom-call | tf_op jit(solution)/shard_map/tail/pallas_call | solution.py:331
  65.9 0.7 broadcast_in_dim.3
  66.6 9.1 %all_to_all.11.parts = bf16[32,8,128]{2,1,0:T(8,128)(2,1)S(1)} all-to-all(bf16[32,8,128]{2,1,0:T(8,128)(2,1)S(1)} %broadcast_in_dim.3), channel_id=1, replica_groups=mesh['fsdp'=2,'layer'=4,'row'=2,'core'=2] {'fsdp','layer','row','core'}, dimensions={0} | all-to-all | bytes 131072 | tf_op jit(solution)/shard_map/all_to_all | solution.py:408
  75.7 0.6 finish.1
  (46 shorter events, 0.5 us)
Async XLA Ops:
  0.6 2.6 %copy-start.5 = (bf16[1,128,3072]{2,1,0:T(8,128)(2,1)S(1)}, bf16[1,128,3072]{2,1,0:T(8,128)(2,1)}, u32[]{:S(2)}) copy-start(bf16[1,128,3072]{2,1,0:T(8,128)(2,1)} %param.9) | copy-start | bytes 2359300
  0.6 2.6 %copy-start.4 = (bf16[1,128,3072]{2,1,0:T(8,128)(2,1)S(1)}, bf16[1,128,3072]{2,1,0:T(8,128)(2,1)}, u32[]{:S(2)}) copy-start(bf16[1,128,3072]{2,1,0:T(8,128)(2,1)} %param.8) | copy-start | bytes 2359300
  1.9 1.9 %collective-permute-start.1 = (bf16[128,1536]{1,0:T(8,128)(2,1)S(1)}, bf16[128,1536]{1,0:T(8,128)(2,1)S(1)}, u32[]{:S(2)}, u32[]{:S(2)}) collective-permute-start(bf16[128,1536]{1,0:T(8,128)(2,1)S(1)} %get-tuple-element.17), channel_id=1, source_target_pairs={{0,1},{1,0},{2,3},{3,2},{4,5},{5,4},{6,7},{7,6},{8,9},{9,8},{10,11... | collective-permute-start | bytes 1179656 | tf_op jit(solution)/shard_map/ppermute | solution.py:400
  2.5 1.9 %collective-permute-start = (bf16[128,1536]{1,0:T(8,128)(2,1)S(1)}, bf16[128,1536]{1,0:T(8,128)(2,1)S(1)}, u32[]{:S(2)}, u32[]{:S(2)}) collective-permute-start(bf16[128,1536]{1,0:T(8,128)(2,1)S(1)} %get-tuple-element.16), channel_id=1, source_target_pairs={{0,1},{1,0},{2,3},{3,2},{4,5},{5,4},{6,7},{7,6},{8,9},{9,8},{10,11... | collective-permute-start | bytes 1179656 | tf_op jit(solution)/shard_map/ppermute | solution.py:400
  3.8 0.9 %copy-start.9 = (bf16[128,1536]{1,0:T(8,128)(2,1)}, bf16[128,1536]{1,0:T(8,128)(2,1)S(1)}, u32[]{:S(2)}) copy-start(bf16[128,1536]{1,0:T(8,128)(2,1)S(1)} %collective-permute-done.1.v_core) | copy-start | bytes 1179652
  4.4 0.7 copy-start.10
  4.4 3.7 %copy-start.6 = (bf16[1,128,3072]{2,1,0:T(8,128)(2,1)S(1)}, bf16[1,128,3072]{2,1,0:T(8,128)(2,1)}, u32[]{:S(2)}) copy-start(bf16[1,128,3072]{2,1,0:T(8,128)(2,1)} %param.7) | copy-start | bytes 2359300
  4.4 5.9 %copy-start.14 = (bf16[1536,1000]{0,1:T(8,128)(2,1)S(1)}, bf16[1536,1000]{0,1:T(8,128)(2,1)}, u32[]{:S(2)}) copy-start(bf16[1536,1000]{0,1:T(8,128)(2,1)} %param.10) | copy-start | bytes 9216004
  5.1 8.8 %collective-permute-start.3 = (bf16[128,768]{1,0:T(8,128)(2,1)S(1)}, bf16[128,768]{1,0:T(8,128)(2,1)S(1)}, u32[]{:S(2)}, u32[]{:S(2)}) collective-permute-start(bf16[128,768]{1,0:T(8,128)(2,1)S(1)} %get-tuple-element.47), channel_id=1, source_target_pairs={{0,2},{2,0},{1,3},{3,1},{4,6},{6,4},{5,7},{7,5},{8,10},{10,8},{9,1... | collective-permute-start | bytes 589832 | tf_op jit(solution)/shard_map/ppermute | solution.py:404
  8.1 14.7 %collective-permute-start.10 = (bf16[128,1536]{1,0:T(8,128)(2,1)S(1)}, bf16[128,1536]{1,0:T(8,128)(2,1)S(1)}, u32[]{:S(2)}, u32[]{:S(2)}) collective-permute-start(bf16[128,1536]{1,0:T(8,128)(2,1)S(1)} %constant_dynamic-slice_fusion), channel_id=1, source_target_pairs={{0,1},{1,0},{2,3},{3,2},{4,5},{5,4},{6,7},{7,6},{8,9},{9,8},{10,11... | collective-permute-start | bytes 1179656 | tf_op jit(solution)/shard_map/ppermute | solution.py:400
  8.2 9.8 %collective-permute-start.2 = (bf16[128,768]{1,0:T(8,128)(2,1)S(1)}, bf16[128,768]{1,0:T(8,128)(2,1)S(1)}, u32[]{:S(2)}, u32[]{:S(2)}) collective-permute-start(bf16[128,768]{1,0:T(8,128)(2,1)S(1)} %get-tuple-element.46), channel_id=1, source_target_pairs={{0,2},{2,0},{1,3},{3,1},{4,6},{6,4},{5,7},{7,5},{8,10},{10,8},{9,1... | collective-permute-start | bytes 589832 | tf_op jit(solution)/shard_map/ppermute | solution.py:404
  8.8 17.6 %collective-permute-start.4 = (bf16[2,128,768]{2,1,0:T(8,128)(2,1)S(1)}, bf16[2,128,768]{2,1,0:T(8,128)(2,1)S(1)}, u32[]{:S(2)}, u32[]{:S(2)}) collective-permute-start(bf16[2,128,768]{2,1,0:T(8,128)(2,1)S(1)} %get-tuple-element.36), channel_id=1, source_target_pairs={{0,2},{2,0},{1,3},{3,1},{4,6},{6,4},{5,7},{7,5},{8,10},{10,8},{9,1... | collective-permute-start | bytes 1179656 | tf_op jit(solution)/shard_map/ppermute | solution.py:404
  10.4 12.4 %copy-start.2 = (bf16[1000,768]{1,0:T(8,128)(2,1)}, bf16[1000,768]{1,0:T(8,128)(2,1)S(1)}, u32[]{:S(2)}) copy-start(bf16[1000,768]{1,0:T(8,128)(2,1)S(1)} %dynamic-slice_bitcast_fusion.part) | copy-start | bytes 4608004
  10.4 24.8 %collective-permute-start.12 = (bf16[1000,768]{1,0:T(8,128)(2,1)S(1)}, bf16[1000,768]{1,0:T(8,128)(2,1)S(1)}, u32[]{:S(2)}, u32[]{:S(2)}) collective-permute-start(bf16[1000,768]{1,0:T(8,128)(2,1)S(1)} %dynamic-slice_bitcast_fusion.part), channel_id=1, source_target_pairs={{0,16},{17,1},{2,18},{19,3},{4,20},{21,5},{6,22},{23,7},{8,24},{25... | collective-permute-start | bytes 4608008 | tf_op jit(solution)/shard_map/ppermute | solution.py:389
  13.9 8.9 %copy-start.7 = (bf16[128,768]{1,0:T(8,128)(2,1)}, bf16[128,768]{1,0:T(8,128)(2,1)S(1)}, u32[]{:S(2)}) copy-start(bf16[128,768]{1,0:T(8,128)(2,1)S(1)} %collective-permute-done.3.first_given) | copy-start | bytes 589828
  14.0 5.9 %collective-permute-start.5 = (bf16[128,768]{1,0:T(8,128)(2,1)S(1)}, bf16[128,768]{1,0:T(8,128)(2,1)S(1)}, u32[]{:S(2)}, u32[]{:S(2)}) collective-permute-start(bf16[128,768]{1,0:T(8,128)(2,1)S(1)} %bitcast_select_fusion), channel_id=1, source_target_pairs={{0,4},{4,0},{8,12},{12,8},{1,5},{5,1},{9,13},{13,9},{2,6},{6,2},{1... | collective-permute-start | bytes 589832 | tf_op jit(solution)/shard_map/ppermute | solution.py:396
  18.0 5.7 %copy-start.8 = (bf16[128,768]{1,0:T(8,128)(2,1)}, bf16[128,768]{1,0:T(8,128)(2,1)S(1)}, u32[]{:S(2)}) copy-start(bf16[128,768]{1,0:T(8,128)(2,1)S(1)} %collective-permute-done.2.first_kept) | copy-start | bytes 589828
  19.9 10.8 %collective-permute-start.8 = (bf16[128,768]{1,0:T(8,128)(2,1)S(1)}, bf16[128,768]{1,0:T(8,128)(2,1)S(1)}, u32[]{:S(2)}, u32[]{:S(2)}) collective-permute-start(bf16[128,768]{1,0:T(8,128)(2,1)S(1)} %fusion.9), channel_id=1, source_target_pairs={{0,8},{4,12},{8,0},{12,4},{1,9},{5,13},{9,1},{13,5},{2,10},{6,14},... | collective-permute-start | bytes 589832 | tf_op jit(solution)/shard_map/ppermute | solution.py:396
  22.8 3.7 %copy-start.12 = (bf16[128,1536]{1,0:T(8,128)(2,1)}, bf16[128,1536]{1,0:T(8,128)(2,1)S(1)}, u32[]{:S(2)}) copy-start(bf16[128,1536]{1,0:T(8,128)(2,1)S(1)} %collective-permute-done.10.q_core) | copy-start | bytes 1179652
  23.7 14.8 %collective-permute-start.11 = (bf16[2,128,768]{2,1,0:T(8,128)(2,1)}, bf16[2,128,768]{2,1,0:T(8,128)(2,1)}, u32[]{:S(2)}, u32[]{:S(2)}) collective-permute-start(bf16[2,128,768]{2,1,0:T(8,128)(2,1)} %pad_maximum_fusion.2), channel_id=1, source_target_pairs={{0,2},{2,0},{1,3},{3,1},{4,6},{6,4},{5,7},{7,5},{8,10},{10,8},{9,1... | collective-permute-start | bytes 1179656 | tf_op jit(solution)/shard_map/ppermute | solution.py:404
  26.4 4.3 %copy-start.11 = (bf16[2,128,768]{2,1,0:T(8,128)(2,1)}, bf16[2,128,768]{2,1,0:T(8,128)(2,1)S(1)}, u32[]{:S(2)}) copy-start(bf16[2,128,768]{2,1,0:T(8,128)(2,1)S(1)} %collective-permute-done.4.kv_last) | copy-start | bytes 1179652
  27.3 7.9 %collective-permute-start.6 = (bf16[128,768]{1,0:T(8,128)(2,1)}, bf16[128,768]{1,0:T(8,128)(2,1)}, u32[]{:S(2)}, u32[]{:S(2)}) collective-permute-start(bf16[128,768]{1,0:T(8,128)(2,1)} %bitcast.27), channel_id=1, source_target_pairs={{0,4},{4,0},{8,12},{12,8},{1,5},{5,1},{9,13},{13,9},{2,6},{6,2},{1... | collective-permute-start | bytes 589832 | tf_op jit(solution)/shard_map/ppermute | solution.py:396
  29.4 6.9 %collective-permute-start.7 = (bf16[128,768]{1,0:T(8,128)(2,1)S(1)}, bf16[128,768]{1,0:T(8,128)(2,1)}, u32[]{:S(2)}, u32[]{:S(2)}) collective-permute-start(bf16[128,768]{1,0:T(8,128)(2,1)S(1)} %bitcast.67), channel_id=1, source_target_pairs={{4,8},{8,4},{5,9},{9,5},{6,10},{10,6},{7,11},{11,7},{20,24},{24,20... | collective-permute-start | bytes 589832 | tf_op jit(solution)/shard_map/ppermute | solution.py:481
  30.8 7.7 %copy-start.13 = (bf16[128,768]{1,0:T(8,128)(2,1)}, bf16[128,768]{1,0:T(8,128)(2,1)S(1)}, u32[]{:S(2)}) copy-start(bf16[128,768]{1,0:T(8,128)(2,1)S(1)} %broadcast_select_fusion.2.kept) | copy-start | bytes 589828
  30.8 7.7 %collective-permute-start.9 = (bf16[128,768]{1,0:T(8,128)(2,1)S(1)}, bf16[128,768]{1,0:T(8,128)(2,1)}, u32[]{:S(2)}, u32[]{:S(2)}) collective-permute-start(bf16[128,768]{1,0:T(8,128)(2,1)S(1)} %broadcast_select_fusion.2.kept), channel_id=1, source_target_pairs={{0,4},{4,0},{8,12},{12,8},{1,5},{5,1},{9,13},{13,9},{2,6},{6,2},{1... | collective-permute-start | bytes 589832 | tf_op jit(solution)/shard_map/ppermute | solution.py:396
  35.2 1.1 %copy-start.3 = (bf16[1000,768]{1,0:T(8,128)(2,1)}, bf16[1000,768]{1,0:T(8,128)(2,1)S(1)}, u32[]{:S(2)}) copy-start(bf16[1000,768]{1,0:T(8,128)(2,1)S(1)} %collective-permute-done.12.part_there) | copy-start | bytes 4608004
  62.4 13.3 %copy-start = (f32[3072]{0:T(1024)S(1)}, f32[3072]{0:T(1024)}, u32[]{:S(2)}) copy-start(f32[3072]{0:T(1024)} %param.12) | copy-start | bytes 36868
  62.4 13.3 %copy-start.1 = (f32[3072]{0:T(1024)S(1)}, f32[3072]{0:T(1024)}, u32[]{:S(2)}) copy-start(f32[3072]{0:T(1024)} %param.13) | copy-start | bytes 36868

commit v2 on v1

--- a/solution.py
+++ b/solution.py
@@ -67,19 +67,25 @@
     return jnp.concatenate([a, b, c, pad], axis=0)
 
 
-def two_heads(q, keys, values, gain_q, gain_k, edge):
+def prepare(q, keys, values, gain_q, gain_k):
     centre, eye = centring()
+    tile = lambda x, t: x[t * HEAD:(t + 1) * HEAD]
+    qn = [(unit_rows(tile(q, t), centre) * gain_q).astype(BF16) for t in range(GROUP)]
+    qns = [jnp.transpose(x) for x in qn]
+    kn = [(unit_rows(tile(keys, t), centre) * gain_k).astype(BF16) for t in range(GROUP + 2)]
+    knt = [jnp.transpose(x) for x in kn]
+    vt = dot(eye, values, NT).astype(BF16)
+    vt = [vt[:, t * HEAD:(t + 1) * HEAD] for t in range(GROUP + 2)]
+    return qn, qns, kn, knt, vt
+
+
+def two_heads(prepared, edge):
+    qn, qns, kn, knt, vt = prepared
     tile = lambda x, t: x[t * HEAD:(t + 1) * HEAD]
     side = lambda x, i: x[:, i * HEAD:(i + 1) * HEAD]
     beside = lambda *parts: jnp.concatenate(parts, axis=1)
     below = lambda *parts: jnp.concatenate(parts, axis=0)
-    qn, qnt, qns = [], [], []
-    for t in range(GROUP):
-        qn.append((unit_rows(tile(q, t), centre) * gain_q).astype(BF16))
-        x = jnp.transpose(qn[t])
-        qns.append(x)
-        qnt.append(two((tile(x, 0), tile(x, 1))))
-    kn = [(unit_rows(tile(keys, t), centre) * gain_k).astype(BF16) for t in range(GROUP + 2)]
+    qnt = [two((tile(x, 0), tile(x, 1))) for x in qns]
 
     last = GROUP + 1
     attn = []
@@ -94,9 +100,6 @@
         expo = jnp.exp2((scores - top) * (SCALE * LOG2E))
         attn.append((expo * (1.0 / jnp.sum(expo, axis=0, keepdims=True))).astype(BF16))
 
-    knt = [jnp.transpose(x) for x in kn]
-    vt = dot(eye, values, NT).astype(BF16)
-    vt = [side(vt, t) for t in range(GROUP + 2)]
     zero = jnp.zeros((HEAD, HEAD), BF16)
     results = []
     for i in range(2):
@@ -135,6 +138,7 @@
     edge = [jnp.where(place[i] == 1, NEG, 0.0) for i in (7, 8)]
     tokens = q.shape[0]
     width = STEP * HEAD
+    wide = PER * HEAD
     steps = PER // STEP
     span = GROUP * tokens + 2 * ROW
     paired = pl.multiple_of((1 - odd_layer) * (span - ROW), ROW)
@@ -143,16 +147,15 @@
     def band(row, core, shift):
         return pl.ds(pl.multiple_of((row * 2 + core) * tokens + shift, ROW), tokens)
 
-    def copies(step, kind, even=True):
-        own = pl.ds(pl.multiple_of((mine * steps + step) * width, width), width)
-        half = pl.ds(pl.multiple_of((row * steps + step) * width, width), width)
-        cols = pl.ds(pl.multiple_of(step * width, width), width)
+    def copies(kind, even=True):
+        own = pl.ds(pl.multiple_of(mine * wide, wide), wide)
+        half = pl.ds(pl.multiple_of(row * wide, wide), wide)
         if kind == 0:
             moves = [
                 (q.at[:, own], band(row, core, 0)),
                 (q_core.at[:, half], band(row, 1 - core, 0)),
-                (q_row.at[0, :, cols], band(1 - row, core, 0)),
-                (q_row.at[1, :, cols], band(1 - row, 1 - core, 0)),
+                (q_row.at[0], band(1 - row, core, 0)),
+                (q_row.at[1], band(1 - row, 1 - core, 0)),
             ]
         else:
             i = kind - 1
@@ -161,16 +164,14 @@
             moves = [
                 (raw.at[:, own], band(row, core, ROW)),
                 (raw_core.at[:, half], band(row, 1 - core, ROW)),
-                (kv_last.at[i, :, cols], band(1 - row, 1 - leading, ROW)),
-                (near.at[i * ROW:(i + 1) * ROW, cols], pl.ds(paired, ROW)),
-                (far.at[i * ROW:(i + 1) * ROW, cols], pl.ds(other, ROW)),
-                (first.at[:, cols], band(1 - row, leading, ROW)),
-                (shared.at[:, cols], pl.ds(span, GBLK)),
+                (kv_last.at[i], band(1 - row, 1 - leading, ROW)),
+                (near.at[i * ROW:(i + 1) * ROW], pl.ds(paired, ROW)),
+                (far.at[i * ROW:(i + 1) * ROW], pl.ds(other, ROW)),
+                (first, band(1 - row, leading, ROW)),
+                (shared, pl.ds(span, GBLK)),
             ]
         buf = (qbuf, kbuf, vbuf)[kind]
-        return [
-            pltpu.make_async_copy(a, buf.at[step, b], sems.at[step, kind, n]) for n, (a, b) in enumerate(moves)
-        ]
+        return [pltpu.make_async_copy(a, buf.at[b], sems.at[kind, n]) for n, (a, b) in enumerate(moves)]
 
     def rows_of(readout):
         return pltpu.make_async_copy(readout, weight, late.at[0])
@@ -179,45 +180,45 @@
         heads = pl.ds(step * STEP, STEP)
         return pltpu.make_async_copy(jbuf.at[heads], jac.at[heads], leave.at[step])
 
-    def start(step):
-        for copy in copies(step, 0):
+    for copy in copies(0):
+        copy.start()
+
+    @pl.when(odd_layer == 0)
+    def _():
+        for copy in copies(1, True) + copies(2, True):
             copy.start()
 
-        @pl.when(odd_layer == 0)
-        def _():
-            for copy in copies(step, 1, True) + copies(step, 2, True):
-                copy.start()
-
-        @pl.when(odd_layer == 1)
-        def _():
-            for copy in copies(step, 1, False) + copies(step, 2, False):
-                copy.start()
-
-    start(0)
-
-    @pl.loop(0, steps)
-    def _(step):
-        @pl.when(step + 1 < steps)
-        def _():
-            start(step + 1)
-
-        @pl.when((step == max(steps - 2, 0)) & (here == 1))
-        def _():
-            rows_of(part).start()
-
-        @pl.when((step == max(steps - 2, 0)) & (here == 0))
-        def _():
-            rows_of(part_there).start()
-
+    @pl.when(odd_layer == 1)
+    def _():
+        for copy in copies(1, False) + copies(2, False):
+            copy.start()
+
+    for copy in copies(0) + copies(1) + copies(2):
+        copy.wait()
+
+    @pl.when(here == 1)
+    def _():
+        rows_of(part).start()
+
+    @pl.when(here == 0)
+    def _():
+        rows_of(part_there).start()
+
+    def ready(step):
         at = [pl.ds(mine * PER + step * STEP + i, 1) for i in range(STEP)]
         pair = [jnp.concatenate([gain[i, :] for i in at], axis=1) for gain in (gain_q, gain_k)]
-        for copy in copies(step, 0) + copies(step, 1) + copies(step, 2):
-            copy.wait()
-        made = two_heads(qbuf[step], kbuf[step], vbuf[step], *pair, edge)
+        cols = slice(step * width, (step + 1) * width)
+        return prepare(qbuf[:, cols], kbuf[:, cols], vbuf[:, cols], *pair)
+
+    prepared = ready(0)
+    for step in range(steps):
+        following = ready(step + 1) if step + 1 < steps else None
+        made = two_heads(prepared, edge)
         for i in range(STEP):
             jbuf[step * STEP + i] = made[i][1]
         jacobian(step).start()
-        pooled[pl.ds(step, 1), :] = jnp.concatenate([x for x, _ in made], axis=1)
+        pooled[step:step + 1, :] = jnp.concatenate([x for x, _ in made], axis=1)
+        prepared = following
 
     rows_of(part).wait()
     sums = jnp.concatenate([pooled[i:i + 1, :] for i in range(steps)], axis=1)
@@ -246,12 +247,12 @@
         out_specs=(VMEM, HBM),
         scratch_shapes=[
             pltpu.VMEM(part.shape, BF16),
-            pltpu.VMEM((steps, GROUP * tokens, width), BF16),
-            pltpu.VMEM((steps, keys, width), BF16),
-            pltpu.VMEM((steps, keys, width), BF16),
+            pltpu.VMEM((GROUP * tokens, PER * HEAD), BF16),
+            pltpu.VMEM((keys, PER * HEAD), BF16),
+            pltpu.VMEM((keys, PER * HEAD), BF16),
             pltpu.VMEM((PER, HEAD, HEAD), F32),
             pltpu.VMEM((8, width), F32),
-            pltpu.SemaphoreType.DMA((steps, 3, 7)),
+            pltpu.SemaphoreType.DMA((3, 7)),
             pltpu.SemaphoreType.DMA((1,)),
             pltpu.SemaphoreType.DMA((steps,)),
         ],

time: 76.8 us -> 76.2 us (level)
  no operation moved by 1% of the time
where the time goes in v2:
time: 76.2 us; the launch traced here: 75.8 us
  blocking collectives  23.1 us (30%)
  starting transfers between devices  22.9 us (30%)
  Pallas kernels  13.5 us (18%)
  waiting for transfers between devices  8.12 us (11%)
  local copies, waits for them, and re-layouts  4.43 us (6%)
  other arithmetic  2.18 us (3%)
  between operations  1.57 us (2%)
    all_to_all x2, blocking collectives, every_device(): return lax.all_to_all(x, ('fsdp', 'layer', 'row', 'core'), 0, 0, tiled=True)  23.1 us
    ppermute x4, starting transfers between devices, xor_layer(): lax.ppermute(x, 'layer', [(i, i ^ bit) for i in range(lax.axis_size('laye...  10.8 us
    pallas_call x1, Pallas kernels, attend(): pl.pallas_call(functools.partial(attend_kernel, count), out_shape=(jax.Sh...  9.41 us
    ppermute x4, starting transfers between devices, other_row(): return lax.ppermute(x, 'row', [(0, 1), (1, 0)])  6.56 us
    ppermute x4, waiting for transfers between devices, xor_layer(): lax.ppermute(x, 'layer', [(i, i ^ bit) for i in range(lax.axis_size('laye...  3.91 us
    ppermute x1, starting transfers between devices, group_readout(): there = lax.ppermute(part, ('fsdp', 'layer', 'row', 'core'), pairs)  3.49 us
    pallas_call x1, Pallas kernels, tail(): pl.pallas_call(functools.partial(tail_kernel, count, classes, views), out...  3.47 us
    ppermute x4, waiting for transfers between devices, other_row(): return lax.ppermute(x, 'row', [(0, 1), (1, 0)])  3.2 us
  transfers between devices with their start and end apart: 13, of which 6 were waited for; matrix products, arithmetic and copies ran while one was open for 4% of the time, Pallas kernels for 0%

profile of v2, /device:TPU:0, one launch (start us, length us, event | category | flops | bytes accessed | tf_op | source)
XLA Modules:
  0.0 75.8 jit_solution(3982622937318440991)
XLA Ops:
  0.7 1.3 %dynamic-slice_bitcast_fusion.1 = (bf16[128,1536]{1,0:T(8,128)(2,1)S(1)}, bf16[128,1536]{1,0:T(8,128)(2,1)S(1)}) fusion(bf16[1,128,3072]{2,1,0:T(8,128)(2,1)} %param.9, s32[]{:T(128)S(6)} %select_n.194, bf16[1,128,3072]{2,1,0:T(8,128)(2,1)} %param.8), kind=kLoop, calls=%fused_computation.15 | loop fusion | bytes 1572868 | tf_op jit(solution)/shard_map/dynamic_slice | solution.py:443
  1.9 0.5 collective-permute-start.1
  3.4 0.4 collective-permute-done.1.v_core
  3.8 0.6 collective-permute-done.k_core
  4.4 0.3 fusion
  4.7 0.4 copy-done.10
  5.1 3.0 %collective-permute-start.3 = (bf16[128,768]{1,0:T(8,128)(2,1)S(1)}, bf16[128,768]{1,0:T(8,128)(2,1)S(1)}, u32[]{:S(2)}, u32[]{:S(2)}) collective-permute-start(bf16[128,768]{1,0:T(8,128)(2,1)S(1)} %get-tuple-element.47), channel_id=1, source_target_pairs={{0,2},{2,0},{1,3},{3,1},{4,6},{6,4},{5,7},{7,5},{8,10},{10,8},{9,1... | collective-permute-start | bytes 589832 | tf_op jit(solution)/shard_map/ppermute | solution.py:405
  8.2 0.6 collective-permute-start.2
  8.8 1.5 %collective-permute-start.4 = (bf16[2,128,768]{2,1,0:T(8,128)(2,1)S(1)}, bf16[2,128,768]{2,1,0:T(8,128)(2,1)S(1)}, u32[]{:S(2)}, u32[]{:S(2)}) collective-permute-start(bf16[2,128,768]{2,1,0:T(8,128)(2,1)S(1)} %get-tuple-element.36), channel_id=1, source_target_pairs={{0,2},{2,0},{1,3},{3,1},{4,6},{6,4},{5,7},{7,5},{8,10},{10,8},{9,1... | collective-permute-start | bytes 1179656 | tf_op jit(solution)/shard_map/ppermute | solution.py:405
  10.3 0.1 dynamic-slice_bitcast_fusion.part
  10.4 3.5 %collective-permute-start.12 = (bf16[1000,768]{1,0:T(8,128)(2,1)S(1)}, bf16[1000,768]{1,0:T(8,128)(2,1)S(1)}, u32[]{:S(2)}, u32[]{:S(2)}) collective-permute-start(bf16[1000,768]{1,0:T(8,128)(2,1)S(1)} %dynamic-slice_bitcast_fusion.part), channel_id=1, source_target_pairs={{0,16},{17,1},{2,18},{19,3},{4,20},{21,5},{6,22},{23,7},{8,24},{25... | collective-permute-start | bytes 4608008 | tf_op jit(solution)/shard_map/ppermute | solution.py:390
  14.0 2.0 %collective-permute-start.5 = (bf16[128,768]{1,0:T(8,128)(2,1)S(1)}, bf16[128,768]{1,0:T(8,128)(2,1)S(1)}, u32[]{:S(2)}, u32[]{:S(2)}) collective-permute-start(bf16[128,768]{1,0:T(8,128)(2,1)S(1)} %bitcast_select_fusion), channel_id=1, source_target_pairs={{0,4},{4,0},{8,12},{12,8},{1,5},{5,1},{9,13},{13,9},{2,6},{6,2},{1... | collective-permute-start | bytes 589832 | tf_op jit(solution)/shard_map/ppermute | solution.py:397
  16.0 2.0 %collective-permute-done.2.first_kept = bf16[128,768]{1,0:T(8,128)(2,1)S(1)} collective-permute-done((bf16[128,768]{1,0:T(8,128)(2,1)S(1)}, bf16[128,768]{1,0:T(8,128)(2,1)S(1)}, u32[]{:S(2)}, u32[]{:S(2)}) %collective-permute-start.2) | collective-permute-done | bytes 196640 | tf_op jit(solution)/shard_map/ppermute | solution.py:405
  18.1 1.8 %collective-permute-done.5 = bf16[128,768]{1,0:T(8,128)(2,1)S(1)} collective-permute-done((bf16[128,768]{1,0:T(8,128)(2,1)S(1)}, bf16[128,768]{1,0:T(8,128)(2,1)S(1)}, u32[]{:S(2)}, u32[]{:S(2)}) %collective-permute-start.5) | collective-permute-done | bytes 196640 | tf_op jit(solution)/shard_map/ppermute | solution.py:397
  19.9 2.9 %collective-permute-start.8 = (bf16[128,768]{1,0:T(8,128)(2,1)S(1)}, bf16[128,768]{1,0:T(8,128)(2,1)S(1)}, u32[]{:S(2)}, u32[]{:S(2)}) collective-permute-start(bf16[128,768]{1,0:T(8,128)(2,1)S(1)} %fusion.9), channel_id=1, source_target_pairs={{0,8},{4,12},{8,0},{12,4},{1,9},{5,13},{9,1},{13,5},{2,10},{6,14},... | collective-permute-start | bytes 589832 | tf_op jit(solution)/shard_map/ppermute | solution.py:397
  22.9 0.9 %pad_maximum_fusion.2 = bf16[2,128,768]{2,1,0:T(8,128)(2,1)} fusion(bf16[1,128,768]{2,1,0:T(8,128)(2,1)S(1)} %dynamic-slice_bitcast_fusion.3, bf16[1,128,768]{2,1,0:T(8,128)(2,1)S(1)} %dynamic-slice_bitcast_fusion.4), kind=kLoop, calls=%fused_computation.14 | loop fusion | flops 196608 | bytes 786432 | tf_op jit(solution)/shard_map/stack | solution.py:486
  23.7 1.5 %collective-permute-start.11 = (bf16[2,128,768]{2,1,0:T(8,128)(2,1)}, bf16[2,128,768]{2,1,0:T(8,128)(2,1)}, u32[]{:S(2)}, u32[]{:S(2)}) collective-permute-start(bf16[2,128,768]{2,1,0:T(8,128)(2,1)} %pad_maximum_fusion.2), channel_id=1, source_target_pairs={{0,2},{2,0},{1,3},{3,1},{4,6},{6,4},{5,7},{7,5},{8,10},{10,8},{9,1... | collective-permute-start | bytes 1179656 | tf_op jit(solution)/shard_map/ppermute | solution.py:405
  25.2 1.2 %collective-permute-done.4.kv_last = bf16[2,128,768]{2,1,0:T(8,128)(2,1)S(1)} collective-permute-done((bf16[2,128,768]{2,1,0:T(8,128)(2,1)S(1)}, bf16[2,128,768]{2,1,0:T(8,128)(2,1)S(1)}, u32[]{:S(2)}, u32[]{:S(2)}) %collective-permute-start.4) | collective-permute-done | bytes 393248 | tf_op jit(solution)/shard_map/ppermute | solution.py:405
  26.4 0.1 broadcast_select_fusion.3
  26.6 0.7 broadcast_select_fusion.4
  27.3 2.1 %collective-permute-start.6 = (bf16[128,768]{1,0:T(8,128)(2,1)}, bf16[128,768]{1,0:T(8,128)(2,1)}, u32[]{:S(2)}, u32[]{:S(2)}) collective-permute-start(bf16[128,768]{1,0:T(8,128)(2,1)} %bitcast.27), channel_id=1, source_target_pairs={{0,4},{4,0},{8,12},{12,8},{1,5},{5,1},{9,13},{13,9},{2,6},{6,2},{1... | collective-permute-start | bytes 589832 | tf_op jit(solution)/shard_map/ppermute | solution.py:397
  29.4 1.3 %collective-permute-start.7 = (bf16[128,768]{1,0:T(8,128)(2,1)S(1)}, bf16[128,768]{1,0:T(8,128)(2,1)}, u32[]{:S(2)}, u32[]{:S(2)}) collective-permute-start(bf16[128,768]{1,0:T(8,128)(2,1)S(1)} %bitcast.67), channel_id=1, source_target_pairs={{4,8},{8,4},{5,9},{9,5},{6,10},{10,6},{7,11},{11,7},{20,24},{24,20... | collective-permute-start | bytes 589832 | tf_op jit(solution)/shard_map/ppermute | solution.py:482
  30.8 3.8 %collective-permute-start.9 = (bf16[128,768]{1,0:T(8,128)(2,1)S(1)}, bf16[128,768]{1,0:T(8,128)(2,1)}, u32[]{:S(2)}, u32[]{:S(2)}) collective-permute-start(bf16[128,768]{1,0:T(8,128)(2,1)S(1)} %broadcast_select_fusion.2.kept), channel_id=1, source_target_pairs={{0,4},{4,0},{8,12},{12,8},{1,5},{5,1},{9,13},{13,9},{2,6},{6,2},{1... | collective-permute-start | bytes 589832 | tf_op jit(solution)/shard_map/ppermute | solution.py:397
  34.6 0.6 stack.97.place
  35.2 1.1 %copy-done.3 = bf16[1000,768]{1,0:T(8,128)(2,1)} copy-done((bf16[1000,768]{1,0:T(8,128)(2,1)}, bf16[1000,768]{1,0:T(8,128)(2,1)S(1)}, u32[]{:S(2)}) %copy-start.3) | copy-done | bytes 1536024
  36.3 2.1 %collective-permute-done.9.there = bf16[128,768]{1,0:T(8,128)(2,1)} collective-permute-done((bf16[128,768]{1,0:T(8,128)(2,1)S(1)}, bf16[128,768]{1,0:T(8,128)(2,1)}, u32[]{:S(2)}, u32[]{:S(2)}) %collective-permute-start.9) | collective-permute-done | bytes 196640 | tf_op jit(solution)/shard_map/ppermute | solution.py:397
  38.5 9.4 %attend.1 = (f32[32,8,128]{2,1,0:T(8,128)}, f32[6,128,128]{2,1,0:T(8,128)}) custom-call(s32[9]{0:T(128)} %stack.97.place, f32[24,128]{1,0:T(8,128)} %bitcast.56, f32[24,128]{1,0:T(8,128)} %bitcast.58, bf16[128,3072]{1,0:T(8,128)(2,1)} %bitcast.62, bf16[128,3072]{1,0:T(8,128)(2,1)} %bitcast.60, bf16[128,3072]{1,0:T(8,128)(2,1)} %bitcast.61, ...), custom_call_target="tpu_custom_call" | custom-call | flops 1200000000 | bytes 6000000 | tf_op jit(solution)/shard_map/attend/pallas_call | solution.py:240
  47.9 13.9 %all_to_all.10.logits = f32[32,8,128]{2,1,0:T(8,128)} all-to-all(f32[32,8,128]{2,1,0:T(8,128)} %get-tuple-element.23), channel_id=1, replica_groups=mesh['fsdp'=2,'layer'=4,'row'=2,'core'=2] {'fsdp','layer','row','core'}, dimensions={0} | all-to-all | bytes 262144 | tf_op jit(solution)/shard_map/all_to_all | solution.py:409
  61.9 3.5 %tail.1 = (f32[1,1]{1,0:T(1,128)}, bf16[8,128]{1,0:T(8,128)(2,1)}) custom-call(s32[9]{0:T(128)} %stack.97.place, f32[32,8,128]{2,1,0:T(8,128)} %all_to_all.10.logits, bf16[1000,768]{1,0:T(8,128)(2,1)} %copy-done.2, bf16[1000,768]{1,0:T(8,128)(2,1)} %copy-done.3, f32[6,128,128]{2,1,0:T(8,128)} %get-tuple-element.24.jac), custom_call_target="tpu_custom_call" | custom-call | tf_op jit(solution)/shard_map/tail/pallas_call | solution.py:332
  65.3 0.7 broadcast_in_dim.3
  66.0 9.1 %all_to_all.11.parts = bf16[32,8,128]{2,1,0:T(8,128)(2,1)S(1)} all-to-all(bf16[32,8,128]{2,1,0:T(8,128)(2,1)S(1)} %broadcast_in_dim.3), channel_id=1, replica_groups=mesh['fsdp'=2,'layer'=4,'row'=2,'core'=2] {'fsdp','layer','row','core'}, dimensions={0} | all-to-all | bytes 131072 | tf_op jit(solution)/shard_map/all_to_all | solution.py:409
  75.1 0.6 finish.1
  (46 shorter events, 0.5 us)
Async XLA Ops:
  0.6 2.6 %copy-start.5 = (bf16[1,128,3072]{2,1,0:T(8,128)(2,1)S(1)}, bf16[1,128,3072]{2,1,0:T(8,128)(2,1)}, u32[]{:S(2)}) copy-start(bf16[1,128,3072]{2,1,0:T(8,128)(2,1)} %param.9) | copy-start | bytes 2359300
  0.6 2.6 %copy-start.4 = (bf16[1,128,3072]{2,1,0:T(8,128)(2,1)S(1)}, bf16[1,128,3072]{2,1,0:T(8,128)(2,1)}, u32[]{:S(2)}) copy-start(bf16[1,128,3072]{2,1,0:T(8,128)(2,1)} %param.8) | copy-start | bytes 2359300
  1.9 1.9 %collective-permute-start.1 = (bf16[128,1536]{1,0:T(8,128)(2,1)S(1)}, bf16[128,1536]{1,0:T(8,128)(2,1)S(1)}, u32[]{:S(2)}, u32[]{:S(2)}) collective-permute-start(bf16[128,1536]{1,0:T(8,128)(2,1)S(1)} %get-tuple-element.17), channel_id=1, source_target_pairs={{0,1},{1,0},{2,3},{3,2},{4,5},{5,4},{6,7},{7,6},{8,9},{9,8},{10,11... | collective-permute-start | bytes 1179656 | tf_op jit(solution)/shard_map/ppermute | solution.py:401
  2.5 1.9 %collective-permute-start = (bf16[128,1536]{1,0:T(8,128)(2,1)S(1)}, bf16[128,1536]{1,0:T(8,128)(2,1)S(1)}, u32[]{:S(2)}, u32[]{:S(2)}) collective-permute-start(bf16[128,1536]{1,0:T(8,128)(2,1)S(1)} %get-tuple-element.16), channel_id=1, source_target_pairs={{0,1},{1,0},{2,3},{3,2},{4,5},{5,4},{6,7},{7,6},{8,9},{9,8},{10,11... | collective-permute-start | bytes 1179656 | tf_op jit(solution)/shard_map/ppermute | solution.py:401
  3.8 0.9 %copy-start.9 = (bf16[128,1536]{1,0:T(8,128)(2,1)}, bf16[128,1536]{1,0:T(8,128)(2,1)S(1)}, u32[]{:S(2)}) copy-start(bf16[128,1536]{1,0:T(8,128)(2,1)S(1)} %collective-permute-done.1.v_core) | copy-start | bytes 1179652
  4.4 0.7 copy-start.10
  4.4 3.7 %copy-start.6 = (bf16[1,128,3072]{2,1,0:T(8,128)(2,1)S(1)}, bf16[1,128,3072]{2,1,0:T(8,128)(2,1)}, u32[]{:S(2)}) copy-start(bf16[1,128,3072]{2,1,0:T(8,128)(2,1)} %param.7) | copy-start | bytes 2359300
  4.4 5.9 %copy-start.14 = (bf16[1536,1000]{0,1:T(8,128)(2,1)S(1)}, bf16[1536,1000]{0,1:T(8,128)(2,1)}, u32[]{:S(2)}) copy-start(bf16[1536,1000]{0,1:T(8,128)(2,1)} %param.10) | copy-start | bytes 9216004
  5.1 8.8 %collective-permute-start.3 = (bf16[128,768]{1,0:T(8,128)(2,1)S(1)}, bf16[128,768]{1,0:T(8,128)(2,1)S(1)}, u32[]{:S(2)}, u32[]{:S(2)}) collective-permute-start(bf16[128,768]{1,0:T(8,128)(2,1)S(1)} %get-tuple-element.47), channel_id=1, source_target_pairs={{0,2},{2,0},{1,3},{3,1},{4,6},{6,4},{5,7},{7,5},{8,10},{10,8},{9,1... | collective-permute-start | bytes 589832 | tf_op jit(solution)/shard_map/ppermute | solution.py:405
  8.1 14.7 %collective-permute-start.10 = (bf16[128,1536]{1,0:T(8,128)(2,1)S(1)}, bf16[128,1536]{1,0:T(8,128)(2,1)S(1)}, u32[]{:S(2)}, u32[]{:S(2)}) collective-permute-start(bf16[128,1536]{1,0:T(8,128)(2,1)S(1)} %constant_dynamic-slice_fusion), channel_id=1, source_target_pairs={{0,1},{1,0},{2,3},{3,2},{4,5},{5,4},{6,7},{7,6},{8,9},{9,8},{10,11... | collective-permute-start | bytes 1179656 | tf_op jit(solution)/shard_map/ppermute | solution.py:401
  8.2 9.8 %collective-permute-start.2 = (bf16[128,768]{1,0:T(8,128)(2,1)S(1)}, bf16[128,768]{1,0:T(8,128)(2,1)S(1)}, u32[]{:S(2)}, u32[]{:S(2)}) collective-permute-start(bf16[128,768]{1,0:T(8,128)(2,1)S(1)} %get-tuple-element.46), channel_id=1, source_target_pairs={{0,2},{2,0},{1,3},{3,1},{4,6},{6,4},{5,7},{7,5},{8,10},{10,8},{9,1... | collective-permute-start | bytes 589832 | tf_op jit(solution)/shard_map/ppermute | solution.py:405
  8.8 17.6 %collective-permute-start.4 = (bf16[2,128,768]{2,1,0:T(8,128)(2,1)S(1)}, bf16[2,128,768]{2,1,0:T(8,128)(2,1)S(1)}, u32[]{:S(2)}, u32[]{:S(2)}) collective-permute-start(bf16[2,128,768]{2,1,0:T(8,128)(2,1)S(1)} %get-tuple-element.36), channel_id=1, source_target_pairs={{0,2},{2,0},{1,3},{3,1},{4,6},{6,4},{5,7},{7,5},{8,10},{10,8},{9,1... | collective-permute-start | bytes 1179656 | tf_op jit(solution)/shard_map/ppermute | solution.py:405
  10.4 12.4 %copy-start.2 = (bf16[1000,768]{1,0:T(8,128)(2,1)}, bf16[1000,768]{1,0:T(8,128)(2,1)S(1)}, u32[]{:S(2)}) copy-start(bf16[1000,768]{1,0:T(8,128)(2,1)S(1)} %dynamic-slice_bitcast_fusion.part) | copy-start | bytes 4608004
  10.4 24.8 %collective-permute-start.12 = (bf16[1000,768]{1,0:T(8,128)(2,1)S(1)}, bf16[1000,768]{1,0:T(8,128)(2,1)S(1)}, u32[]{:S(2)}, u32[]{:S(2)}) collective-permute-start(bf16[1000,768]{1,0:T(8,128)(2,1)S(1)} %dynamic-slice_bitcast_fusion.part), channel_id=1, source_target_pairs={{0,16},{17,1},{2,18},{19,3},{4,20},{21,5},{6,22},{23,7},{8,24},{25... | collective-permute-start | bytes 4608008 | tf_op jit(solution)/shard_map/ppermute | solution.py:390
  13.9 8.9 %copy-start.7 = (bf16[128,768]{1,0:T(8,128)(2,1)}, bf16[128,768]{1,0:T(8,128)(2,1)S(1)}, u32[]{:S(2)}) copy-start(bf16[128,768]{1,0:T(8,128)(2,1)S(1)} %collective-permute-done.3.first_given) | copy-start | bytes 589828
  14.0 5.9 %collective-permute-start.5 = (bf16[128,768]{1,0:T(8,128)(2,1)S(1)}, bf16[128,768]{1,0:T(8,128)(2,1)S(1)}, u32[]{:S(2)}, u32[]{:S(2)}) collective-permute-start(bf16[128,768]{1,0:T(8,128)(2,1)S(1)} %bitcast_select_fusion), channel_id=1, source_target_pairs={{0,4},{4,0},{8,12},{12,8},{1,5},{5,1},{9,13},{13,9},{2,6},{6,2},{1... | collective-permute-start | bytes 589832 | tf_op jit(solution)/shard_map/ppermute | solution.py:397
  18.0 5.7 %copy-start.8 = (bf16[128,768]{1,0:T(8,128)(2,1)}, bf16[128,768]{1,0:T(8,128)(2,1)S(1)}, u32[]{:S(2)}) copy-start(bf16[128,768]{1,0:T(8,128)(2,1)S(1)} %collective-permute-done.2.first_kept) | copy-start | bytes 589828
  19.9 10.8 %collective-permute-start.8 = (bf16[128,768]{1,0:T(8,128)(2,1)S(1)}, bf16[128,768]{1,0:T(8,128)(2,1)S(1)}, u32[]{:S(2)}, u32[]{:S(2)}) collective-permute-start(bf16[128,768]{1,0:T(8,128)(2,1)S(1)} %fusion.9), channel_id=1, source_target_pairs={{0,8},{4,12},{8,0},{12,4},{1,9},{5,13},{9,1},{13,5},{2,10},{6,14},... | collective-permute-start | bytes 589832 | tf_op jit(solution)/shard_map/ppermute | solution.py:397
  22.8 3.7 %copy-start.12 = (bf16[128,1536]{1,0:T(8,128)(2,1)}, bf16[128,1536]{1,0:T(8,128)(2,1)S(1)}, u32[]{:S(2)}) copy-start(bf16[128,1536]{1,0:T(8,128)(2,1)S(1)} %collective-permute-done.10.q_core) | copy-start | bytes 1179652
  23.7 14.8 %collective-permute-start.11 = (bf16[2,128,768]{2,1,0:T(8,128)(2,1)}, bf16[2,128,768]{2,1,0:T(8,128)(2,1)}, u32[]{:S(2)}, u32[]{:S(2)}) collective-permute-start(bf16[2,128,768]{2,1,0:T(8,128)(2,1)} %pad_maximum_fusion.2), channel_id=1, source_target_pairs={{0,2},{2,0},{1,3},{3,1},{4,6},{6,4},{5,7},{7,5},{8,10},{10,8},{9,1... | collective-permute-start | bytes 1179656 | tf_op jit(solution)/shard_map/ppermute | solution.py:405
  26.4 4.3 %copy-start.11 = (bf16[2,128,768]{2,1,0:T(8,128)(2,1)}, bf16[2,128,768]{2,1,0:T(8,128)(2,1)S(1)}, u32[]{:S(2)}) copy-start(bf16[2,128,768]{2,1,0:T(8,128)(2,1)S(1)} %collective-permute-done.4.kv_last) | copy-start | bytes 1179652
  27.3 7.9 %collective-permute-start.6 = (bf16[128,768]{1,0:T(8,128)(2,1)}, bf16[128,768]{1,0:T(8,128)(2,1)}, u32[]{:S(2)}, u32[]{:S(2)}) collective-permute-start(bf16[128,768]{1,0:T(8,128)(2,1)} %bitcast.27), channel_id=1, source_target_pairs={{0,4},{4,0},{8,12},{12,8},{1,5},{5,1},{9,13},{13,9},{2,6},{6,2},{1... | collective-permute-start | bytes 589832 | tf_op jit(solution)/shard_map/ppermute | solution.py:397
  29.4 6.9 %collective-permute-start.7 = (bf16[128,768]{1,0:T(8,128)(2,1)S(1)}, bf16[128,768]{1,0:T(8,128)(2,1)}, u32[]{:S(2)}, u32[]{:S(2)}) collective-permute-start(bf16[128,768]{1,0:T(8,128)(2,1)S(1)} %bitcast.67), channel_id=1, source_target_pairs={{4,8},{8,4},{5,9},{9,5},{6,10},{10,6},{7,11},{11,7},{20,24},{24,20... | collective-permute-start | bytes 589832 | tf_op jit(solution)/shard_map/ppermute | solution.py:482
  30.8 7.7 %copy-start.13 = (bf16[128,768]{1,0:T(8,128)(2,1)}, bf16[128,768]{1,0:T(8,128)(2,1)S(1)}, u32[]{:S(2)}) copy-start(bf16[128,768]{1,0:T(8,128)(2,1)S(1)} %broadcast_select_fusion.2.kept) | copy-start | bytes 589828
  30.8 7.7 %collective-permute-start.9 = (bf16[128,768]{1,0:T(8,128)(2,1)S(1)}, bf16[128,768]{1,0:T(8,128)(2,1)}, u32[]{:S(2)}, u32[]{:S(2)}) collective-permute-start(bf16[128,768]{1,0:T(8,128)(2,1)S(1)} %broadcast_select_fusion.2.kept), channel_id=1, source_target_pairs={{0,4},{4,0},{8,12},{12,8},{1,5},{5,1},{9,13},{13,9},{2,6},{6,2},{1... | collective-permute-start | bytes 589832 | tf_op jit(solution)/shard_map/ppermute | solution.py:397
  35.2 1.1 %copy-start.3 = (bf16[1000,768]{1,0:T(8,128)(2,1)}, bf16[1000,768]{1,0:T(8,128)(2,1)S(1)}, u32[]{:S(2)}) copy-start(bf16[1000,768]{1,0:T(8,128)(2,1)S(1)} %collective-permute-done.12.part_there) | copy-start | bytes 4608004
  61.8 13.3 %copy-start = (f32[3072]{0:T(1024)S(1)}, f32[3072]{0:T(1024)}, u32[]{:S(2)}) copy-start(f32[3072]{0:T(1024)} %param.12) | copy-start | bytes 36868
  61.8 13.3 %copy-start.1 = (f32[3072]{0:T(1024)S(1)}, f32[3072]{0:T(1024)}, u32[]{:S(2)}) copy-start(f32[3072]{0:T(1024)} %param.13) | copy-start | bytes 36868
